TPU v7x, 128 devices: a whole 4x4x4 slice. The times are simulated.
128 devices in a mesh: grp: 8 (over y, core), tp: 16 (over z, x).
Axes of the slice: x: 4, y: 4, z: 4, core: 2. Of those that a mesh axis runs over, the one named last changes fastest.
Arguments:
- neighbour_ids: int32 [256, 128], replicated, may hold values from 0 to 15999
- neighbour_shard: int32 [256, 128, 1], replicated, may hold values from 0 to 7; in each aligned block of 4096 rows (0 to 4095, 4096 to 8191, ..., all dimensions but the last counted through in order) at most 1024 rows name the same one
- neighbour_count: int32 [64], replicated, may hold values from 1 to 4
- slot_beam: int32 [64], replicated, may hold values from 0 to 63, each once
- prefix_length: int32 [64], P('grp'), may hold values from 2 to 512
- embed_table: bfloat16 [128000, 2048], P('grp', 'tp')
- encoder_gain: float32 [2048], replicated, may hold values from 0.1 to 1.9
- hidden_in: bfloat16 [64, 8192], P('grp'), may hold values from -6 to 6
- decoder_gain: float32 [8192], replicated, may hold values from 0.1 to 1.9
- fresh_projections: bfloat16 [64, 3, 4096], P('grp', None, 'tp')
- cached_pairs: bfloat16 [64, 2, 512, 4096], P('grp', None, None, 'tp')
- w_self_out: bfloat16 [4096, 8192], P('tp'), may hold values from -0.375 to 0.375
- w_query: bfloat16 [8192, 4096], P(None, 'tp')
- w_pairs: bfloat16 [2048, 2, 4096], P(None, None, 'tp')
- w_cross_out: bfloat16 [4096, 8192], P('tp'), may hold values from -0.375 to 0.375
Outputs:
- self_delta: bfloat16 [64, 8192], P('grp')
- cross_delta: bfloat16 [64, 8192], P('grp')
Inputs may be any that keep to these rules, and one draw needn't show every extreme that they name: `neighbour_shard`: in each aligned block of 4096 rows (slots in order, positions within a slot; block g holds the neighbours of beams 8g to 8g+7), at most 1024 rows name any one shard, a bound that some block reaches.
All inputs are finite; a program needn't handle non-finite values.
Results may differ from a plain program's by a relative error of at most 0.012.
The roundings to bfloat16 on the way count: a program that leaves them out, or rounds other values in their place, can miss the bound.
Values may be sent and summed in bfloat16 or wider, within the bound.
A program may use at most 128 MiB of HBM per device.

v0:
```python
import math

import jax
import jax.numpy as jnp
from jax import lax
from jax.sharding import PartitionSpec as P

HD = 128
DE = 2048
NLEN = 128
KMAX = 4
CACHE = 512


epsilon = 1e-05


def masked_softmax(scores, live_mask):
    masked = jnp.where(live_mask, scores, -jnp.inf)
    maximum = jnp.max(masked, axis=-1, keepdims=True)
    raised = jnp.exp(masked - maximum)
    return raised / jnp.sum(raised, axis=-1, keepdims=True)


def dense_rows(shard_ids, offset_ids, group_index, embed_table):
    inside = shard_ids.reshape(-1) == group_index
    looked = jnp.take(embed_table, offset_ids.reshape(-1), axis=0)
    return jnp.where(inside[:, None], looked, jnp.zeros_like(looked))


def local(
    neighbour_ids,
    neighbour_shard,
    neighbour_count,
    slot_beam,
    prefix_length,
    embed_table,
    encoder_gain,
    hidden_in,
    decoder_gain,
    fresh_projections,
    cached_pairs,
    w_self_out,
    w_query,
    w_pairs,
    w_cross_out,
):
    group_index = lax.axis_index("grp")
    lane_index = lax.axis_index("tp")
    beam_local = hidden_in.shape[0]
    beam_total = slot_beam.shape[0]
    width_local = embed_table.shape[1]
    heads_local = fresh_projections.shape[2] // HD
    span_rows = KMAX * NLEN
    inverse_root = 1.0 / math.sqrt(HD)
    own_beams = lax.dynamic_slice_in_dim(slot_beam, group_index * beam_local, beam_local)
    shard_ids = neighbour_shard.reshape(neighbour_ids.shape)
    partial_rows = dense_rows(shard_ids, neighbour_ids, group_index, embed_table)
    embedded = lax.psum_scatter(partial_rows, "grp", scatter_dimension=0, tiled=True).astype(
        jnp.float32
    )
    squares = lax.psum(jnp.sum(embedded * embedded, axis=1), "tp")
    gain_local = lax.dynamic_slice_in_dim(encoder_gain, lane_index * width_local, width_local)
    encoded = (embedded * lax.rsqrt(squares / DE + epsilon)[:, None] * gain_local[None, :]).astype(
        jnp.bfloat16
    )
    encoded = encoded.reshape(beam_local, span_rows, width_local)
    everyone = lax.all_gather(encoded, "grp", axis=0, tiled=True)
    picked = jnp.take(everyone, own_beams, axis=0)
    flat_rows = picked.reshape(beam_local * span_rows, width_local)
    pair_matrix = w_pairs.reshape(w_pairs.shape[0], -1)
    pair_sums = jnp.dot(
        lax.all_gather(flat_rows, "tp", axis=1, tiled=True),
        pair_matrix,
        preferred_element_type=jnp.float32,
    )
    cross_pairs = pair_sums.astype(jnp.bfloat16).reshape(beam_local, span_rows, 2, heads_local, HD)
    fresh_rows = fresh_projections.reshape(beam_local, 3, heads_local, HD)
    cached = cached_pairs.reshape(beam_local, 2, CACHE, heads_local, HD)
    old_scores = (
        jnp.einsum(
            "bhd,bphd->bhp", fresh_rows[:, 0], cached[:, 0], preferred_element_type=jnp.float32
        )
        * inverse_root
    )
    new_scores = (
        jnp.einsum(
            "bhd,bhd->bh", fresh_rows[:, 0], fresh_rows[:, 1], preferred_element_type=jnp.float32
        )
        * inverse_root
    )
    positions = jnp.arange(CACHE, dtype=jnp.int32)
    live_old = jnp.broadcast_to(
        positions[None, None, :] < prefix_length[:, None, None], old_scores.shape
    )
    live_mask = jnp.concatenate([live_old, jnp.ones(new_scores.shape + (1,), dtype=bool)], axis=-1)
    weights = masked_softmax(
        jnp.concatenate([old_scores, new_scores[..., None]], axis=-1), live_mask
    ).astype(jnp.bfloat16)
    attended = jnp.einsum(
        "bhp,bphd->bhd", weights[..., :CACHE], cached[:, 1], preferred_element_type=jnp.float32
    )
    attended = attended + weights[..., CACHE:].astype(jnp.float32) * fresh_rows[:, 2].astype(
        jnp.float32
    )
    attended = attended.astype(jnp.bfloat16).reshape(beam_local, heads_local * HD)
    self_full = lax.psum(jnp.dot(attended, w_self_out, preferred_element_type=jnp.float32), "tp")
    residual = hidden_in.astype(jnp.float32) + self_full
    normed = (
        residual
        * lax.rsqrt(jnp.mean(residual * residual, axis=-1, keepdims=True) + epsilon)
        * decoder_gain[None, :]
    ).astype(jnp.bfloat16)
    cross_query = (
        jnp.dot(normed, w_query, preferred_element_type=jnp.float32)
        .astype(jnp.bfloat16)
        .reshape(beam_local, heads_local, HD)
    )
    beam_numbers = jnp.arange(beam_total, dtype=jnp.int32)
    counts = jnp.sum(
        jnp.where(own_beams[:, None] == beam_numbers[None, :], neighbour_count[None, :], 0), axis=1
    )
    token_numbers = jnp.arange(span_rows, dtype=jnp.int32)
    cross_scores = (
        jnp.einsum(
            "bhd,bthd->bht", cross_query, cross_pairs[:, :, 0], preferred_element_type=jnp.float32
        )
        * inverse_root
    )
    cross_live = (token_numbers[None, :] < counts[:, None] * NLEN)[:, None, :]
    cross_weights = masked_softmax(cross_scores, cross_live).astype(jnp.bfloat16)
    cross_attended = jnp.einsum(
        "bht,bthd->bhd", cross_weights, cross_pairs[:, :, 1], preferred_element_type=jnp.float32
    )
    cross_attended = cross_attended.astype(jnp.bfloat16).reshape(beam_local, heads_local * HD)
    cross_full = lax.psum(
        jnp.dot(cross_attended, w_cross_out, preferred_element_type=jnp.float32), "tp"
    )
    return (self_full.astype(jnp.bfloat16), cross_full.astype(jnp.bfloat16))


def solution(mesh):
    placed = (
        P(),
        P(),
        P(),
        P(),
        P("grp"),
        P("grp", "tp"),
        P(),
        P("grp", None),
        P(),
        P("grp", None, "tp"),
        P("grp", None, None, "tp"),
        P("tp", None),
        P(None, "tp"),
        P(None, None, "tp"),
        P("tp", None),
    )
    return jax.shard_map(
        local,
        mesh=mesh,
        in_specs=placed,
        out_specs=(P("grp", None), P("grp", None)),
        check_vma=False,
    )
```

profile of v0, /device:TPU:0, one launch (start us, length us, event | category | flops | bytes accessed | tf_op | source)
XLA Modules:
  0.0 598.7 jit_solution(11108862117370845313)
XLA Ops:
  9.0 1.0 compare_select_fusion
  10.1 1.3 compare_reduce_fusion
  11.4 112.1 %gather_fusion = bf16[32768,128]{1,0:T(8,128)(2,1)} fusion(bf16[16000,128]{1,0:T(8,128)(2,1)} %param.20, s32[32768]{0:T(1024)S(1)} %broadcast_clamp_fusion), kind=kCustom, calls=%fused_computation | custom fusion | bytes 16908288 | tf_op jit(solution)/shard_map/jit(_take)/gather | solution.py:27
  123.5 13.2 %select_select_fusion = bf16[32768,128]{1,0:T(8,128)(2,1)} fusion(bf16[32768,128]{1,0:T(8,128)(2,1)} %gather_fusion, pred[32768]{0:T(1024)(128)(4,1)S(1)} %compare_and_fusion, pred[32768]{0:T(1024)(128)(4,1)S(1)} %bitcast.86), kind=kLoop, calls=%fused_computation.5 | loop fusion | flops 8388608 | bytes 16842752 | tf_op jit(solution)/shard_map/jit(_where)/select_n | solution.py:28
  137.5 54.2 %reduce-scatter.2.cloned.1.call-done = bf16[4096,128]{1,0:T(8,128)(2,1)} async-done(((bf16[32768,128]{1,0:T(8,128)(2,1)}), bf16[4096,128]{1,0:T(8,128)(2,1)}) %reduce-scatter.2.cloned.1.call-update) | async-done | bytes 1048592 | tf_op jit(solution)/shard_map/reduce_scatter | solution.py:59
  191.7 1.8 fusion.3
  193.6 74.5 %psum.22 = f32[4096]{0:T(1024)S(1)} all-reduce(f32[4096]{0:T(1024)S(1)} %fusion.3), channel_id=1, replica_groups=mesh['grp'=8,'tp'=16] {'tp'}, use_global_device_ids=true, to_apply=%region_7.8 | all-reduce | flops 4096 | bytes 32768 | tf_op jit(solution)/shard_map/psum | solution.py:62
  268.1 2.6 fusion.5
  270.8 7.1 %reshape.144 = bf16[8,2,512,2,128]{4,3,2,1,0:T(2,128)(2,1)} reshape(bf16[8,2,512,256]{3,2,1,0:T(8,128)(2,1)} %param.25) | data formatting | bytes 8388608 | tf_op jit(solution)/shard_map/reshape | solution.py:79
  278.1 4.7 slice_bitcast_fusion.3
  285.1 1.4 fusion.40
  286.9 27.7 %all-gather.3.cloned.1.call-done = bf16[64,512,128]{2,1,0:T(8,128)(2,1)} async-done(((bf16[8,512,128]{2,1,0:T(8,128)(2,1)}), bf16[64,512,128]{2,1,0:T(8,128)(2,1)}) %all-gather.3.cloned.1.call-update) | async-done | bytes 8388624 | tf_op jit(solution)/shard_map/all_gather | solution.py:68
  314.7 4.1 gather_fusion.1
  318.8 2.9 bitcast_select_fusion
  321.8 1.8 copy.37
  323.9 41.1 %all-reduce.4.cloned.1.call-done = f32[8,8192]{1,0:T(8,128)} async-done(((f32[8,8192]{1,0:T(8,128)}), f32[8,8192]{1,0:T(8,128)}) %all-reduce.4.cloned.1.call-update) | async-done | bytes 262160 | tf_op jit(solution)/shard_map/psum | solution.py:107
  365.0 1.8 multiply_reduce_fusion
  366.8 3.0 fusion.21
  369.8 117.0 %all-gather.5.cloned.1.call-done = bf16[4096,2048]{1,0:T(8,128)(2,1)} async-done(((bf16[4096,128]{1,0:T(8,128)(2,1)}), bf16[4096,2048]{1,0:T(8,128)(2,1)}) %all-gather.5.cloned.1.call-update) | async-done | bytes 16777232 | tf_op jit(solution)/shard_map/all_gather | solution.py:73
  486.8 13.7 %convolution_convert_fusion = bf16[4096,512]{1,0:T(8,128)(2,1)} fusion(bf16[4096,2048]{1,0:T(8,128)(2,1)} %all-gather.5.cloned.1.call-done, bf16[2048,512]{1,0:T(8,128)(2,1)S(1)} %bitcast.83), kind=kOutput, calls=%fused_computation.6 | convolution fusion | flops 8592031744 | bytes 23068672 | tf_op jit(solution)/shard_map/dot_general | solution.py:72
  500.6 6.9 %reshape.151 = bf16[8,512,2,2,128]{4,3,2,1,0:T(2,128)(2,1)} reshape(bf16[4096,512]{1,0:T(8,128)(2,1)} %convolution_convert_fusion) | data formatting | bytes 8388608 | tf_op jit(solution)/shard_map/reshape | solution.py:77
  507.5 4.7 slice_bitcast_fusion.1
  513.4 2.8 fusion.42
  516.3 75.0 %all-reduce.5 = bf16[8,8192]{1,0:T(8,128)(2,1)} all-reduce(f32[8,8192]{1,0:T(8,128)S(1)} %fusion.42), channel_id=1, replica_groups=mesh['grp'=8,'tp'=16] {'tp'}, use_global_device_ids=true, to_apply=%region_10.11 | all-reduce | flops 65536 | bytes 393216 | tf_op jit(solution)/shard_map/psum | solution.py:136
  (56 shorter events, 6.4 us)
Async XLA Ops:
  8.0 183.7 %reduce-scatter.2.cloned.1.call-start = ((), (), s32[]{:S(2)}) async-start(), calls=%async_computation.2 | async-start | bytes 9437184 | tf_op jit(solution)/shard_map/reduce_scatter | solution.py:59
  136.7 178.0 %all-gather.3.cloned.1.call-start = ((), (), s32[]{:S(2)}) async-start(), calls=%async_computation.3 | async-start | bytes 9437184 | tf_op jit(solution)/shard_map/all_gather | solution.py:68
  270.7 7.2 %copy-start.5 = (bf16[8,3,256]{2,0,1:T(8,128)(2,1)S(1)}, bf16[8,3,256]{2,0,1:T(8,128)(2,1)}, u32[]{:S(2)}) copy-start(bf16[8,3,256]{2,0,1:T(8,128)(2,1)} %param.24) | copy-start | bytes 36868
  270.7 7.3 %copy-start.6 = (s32[8]{0:T(128)S(1)}, s32[8]{0:T(128)}, u32[]{:S(2)}) copy-start(s32[8]{0:T(128)} %param.19) | copy-start | bytes 100
  270.7 94.3 %all-reduce.4.cloned.1.call-start = ((), (), s32[]{:S(2)}) async-start(), calls=%async_computation.1 | async-start | bytes 524288 | tf_op jit(solution)/shard_map/psum | solution.py:107
  282.8 2.3 copy-start
  282.8 3.9 copy-start.7
  285.1 36.7 %copy-start.1 = (bf16[2048,2,256]{2,1,0:T(2,128)(2,1)S(1)}, bf16[2048,2,256]{2,1,0:T(2,128)(2,1)}, u32[]{:S(2)}) copy-start(bf16[2048,2,256]{2,1,0:T(2,128)(2,1)} %param.28) | copy-start | bytes 6291460
  286.5 200.4 %all-gather.5.cloned.1.call-start = ((), (), s32[]{:S(2)}) async-start(), calls=%async_computation.4 | async-start | bytes 17825792 | tf_op jit(solution)/shard_map/all_gather | solution.py:73
  318.8 4.8 copy-start.8
  318.8 46.2 %copy-start.3 = (bf16[8,8192]{1,0:T(8,128)(2,1)S(1)}, bf16[8,8192]{1,0:T(8,128)(2,1)}, u32[]{:S(2)}) copy-start(bf16[8,8192]{1,0:T(8,128)(2,1)} %param.22) | copy-start | bytes 393220
  318.8 48.0 %copy-start.4 = (f32[8192]{0:T(1024)S(1)}, f32[8192]{0:T(1024)}, u32[]{:S(2)}) copy-start(f32[8192]{0:T(1024)} %param.23) | copy-start | bytes 98308
  323.6 163.3 %copy-start.2 = (bf16[256,8,2,256]{3,1,2,0:T(8,128)(2,1)S(1)}, bf16[256,8,2,256]{3,1,2,0:T(8,128)(2,1)}, u32[]{:S(2)}) copy-start(bf16[256,8,2,256]{3,1,2,0:T(8,128)(2,1)} %copy.37) | copy-start | bytes 6291460
Sparse Core Ops, SparseCore 0:
  136.8 54.8 reduce-scatter.1
  270.8 43.8 all-gather.2
Sparse Core Ops, SparseCore 1:
  286.6 78.3 all-reduce.3
  367.2 119.6 all-gather.4
where the time goes:
time: 600 us; the launch traced here: 599 us
  waiting for transfers between devices  240 us (40%)
  blocking collectives  149 us (25%)
  local copies, waits for them, and re-layouts  143 us (24%)
  other arithmetic  27 us (4%)
  matrix products  23 us (4%)
  between operations  15.7 us (3%)
    all_gather x1, waiting for transfers between devices, local(): lax.all_gather(flat_rows, 'tp', axis=1, tiled=True)  117 us
    gather x1, local copies, waits for them, and re-layouts, dense_rows(): looked = jnp.take(embed_table, offset_ids.reshape(-1), axis=0)  112 us
    psum x1, blocking collectives, local(): lax.psum(jnp.dot(cross_attended, w_cross_out, preferred_element_type=jnp....  75 us
    psum x1, blocking collectives, local(): squares = lax.psum(jnp.sum(embedded * embedded, axis=1), 'tp')  74.5 us
    reduce_scatter x1, waiting for transfers between devices, local(): lax.psum_scatter(partial_rows, 'grp', scatter_dimension=0, tiled=True)  54.2 us
    psum x1, waiting for transfers between devices, local(): lax.psum(jnp.dot(attended, w_self_out, preferred_element_type=jnp.float32...  41.1 us
    all_gather x1, waiting for transfers between devices, local(): everyone = lax.all_gather(encoded, 'grp', axis=0, tiled=True)  27.7 us
    dot_general x1, matrix products, local(): jnp.dot(lax.all_gather(flat_rows, 'tp', axis=1, tiled=True), pair_matrix,...  13.7 us
  transfers between devices with their start and end apart: 4, of which 4 were waited for; matrix products, arithmetic and copies ran while one was open for 5% of the time, Pallas kernels for 0%

commit v1 on v0

v1 whole, which is shorter than its diff:
```python
import functools
import math

import jax
import jax.numpy as jnp
from jax import lax
from jax.experimental import pallas as pl
from jax.experimental.pallas import tpu as pltpu
from jax.sharding import PartitionSpec as P

MESH = pl.DeviceIdType.MESH
DMA = pltpu.SemaphoreType.DMA
VMEM = pl.BlockSpec(memory_space=pltpu.VMEM)
SMEM = pl.BlockSpec(memory_space=pltpu.SMEM)
ANY = pl.BlockSpec(memory_space=pl.ANY)

HD = 128
DE = 2048
NLEN = 128
KMAX = 4
CACHE = 512
CAP = 1024
GROUPS = 8
LANES = 16
ROOT = 1.0 / math.sqrt(HD)
epsilon = 1e-05
f32 = jnp.float32
bf16 = jnp.bfloat16
BIG = 56 * 2**20


def params(cid=None):
    if cid is None:
        return pltpu.CompilerParams(vmem_limit_bytes=BIG)
    return pltpu.CompilerParams(collective_id=cid, has_side_effects=True, vmem_limit_bytes=BIG)


def remote(src, dst, send, recv, where):
    return pltpu.make_async_remote_copy(
        src_ref=src, dst_ref=dst, send_sem=send, recv_sem=recv, device_id=where, device_id_type=MESH
    )


def greet(peers):
    barrier = pltpu.get_barrier_semaphore()
    for peer in peers:
        pl.semaphore_signal(barrier, inc=1, device_id=peer, device_id_type=MESH)
    pl.semaphore_wait(barrier, len(peers))


def prepare(ids, shards, counts, me):
    slots = jnp.arange(ids.shape[0], dtype=jnp.int32)
    alive = (slots % KMAX) < jnp.repeat(counts, KMAX)
    upper = jnp.triu(jnp.ones((NLEN, NLEN), bf16))
    chunks = ids.shape[0] // GROUPS
    strict = jnp.triu(jnp.ones((chunks, chunks), bf16), 1)

    def ranks(mask):
        inner = jnp.dot(mask.astype(bf16), upper, preferred_element_type=f32)
        before = jnp.dot(inner[..., -1].astype(bf16), strict, preferred_element_type=f32)
        return (inner + before[..., None]).astype(jnp.int32) - 1

    mine = ((shards == me) & alive[:, None]).reshape(GROUPS, chunks, NLEN)
    rank = ranks(mine)
    high, low = rank // 32, rank % 32
    small = jnp.arange(32, dtype=jnp.int32)
    rows = chunks * NLEN
    first = ((high[..., None] == small) & mine[..., None]).astype(bf16).reshape(GROUPS, rows, 32)
    second = low[..., None] == small
    ids3 = ids.reshape(GROUPS, chunks, NLEN)
    parts = jnp.concatenate(
        [
            jnp.where(second, (ids3 // 128)[..., None], 0),
            jnp.where(second, (ids3 % 128)[..., None], 0),
        ],
        axis=-1,
    ).astype(bf16)
    both = jnp.einsum(
        "gra,grb->gab", first, parts.reshape(GROUPS, rows, 64), preferred_element_type=f32
    )
    wanted = (both[..., :32] * 128.0 + both[..., 32:]).astype(jnp.int32).reshape(GROUPS * CAP)
    filled = jnp.sum(mine.astype(jnp.int32), axis=(1, 2))
    own_shards = lax.dynamic_slice_in_dim(shards, me * chunks, chunks)
    own_alive = lax.dynamic_slice_in_dim(alive, me * chunks, chunks)
    holder = jnp.arange(GROUPS, dtype=jnp.int32)[:, None, None]
    named = (own_shards[None] == holder) & own_alive[None, :, None]
    place = jnp.sum(jnp.where(named, ranks(named) + holder * CAP, 0), axis=0).reshape(rows)
    return wanted, filled, place


def look_kernel(wanted, filled, table, out, wide, found):
    step = 1600

    def widen(i, c):
        at = pl.ds(pl.multiple_of(i * step, step), step)
        wide[at, :] = table[at, :].astype(f32)
        return c

    lax.fori_loop(0, table.shape[0] // step, widen, 0)

    def block(g, c):
        base = g * CAP

        def sixteen(k, c):
            for u in range(16):
                found[k * 16 + u, :] = wide[wanted[base + k * 16 + u], :]
            return c

        lax.fori_loop(0, jnp.maximum((filled[g] + 15) // 16, 1), sixteen, 0)
        out[g] = found[...].astype(bf16)
        return c

    lax.fori_loop(0, GROUPS, block, 0)


def look(wanted, filled, table):
    return pl.pallas_call(
        look_kernel,
        out_shape=jax.ShapeDtypeStruct((GROUPS, CAP, table.shape[1]), bf16),
        in_specs=[SMEM, SMEM, VMEM],
        out_specs=VMEM,
        scratch_shapes=[pltpu.VMEM(table.shape, f32), pltpu.VMEM((CAP, table.shape[1]), f32)],
        compiler_params=params(),
        name="look",
    )(wanted, filled, table)


def place_kernel(place, got, out, wide, found):
    for g in range(GROUPS):
        wide[pl.ds(g * CAP, CAP), :] = got[g].astype(f32)

    def pair(p, c):
        base = p * 1024

        def sixteen(k, c):
            for u in range(16):
                found[k * 16 + u, :] = wide[place[base + k * 16 + u], :]
            return c

        lax.fori_loop(0, 64, sixteen, 0)
        out[p] = found[...].astype(bf16)
        return c

    lax.fori_loop(0, 4, pair, 0)


def put_in_place(place, got):
    return pl.pallas_call(
        place_kernel,
        out_shape=jax.ShapeDtypeStruct((4, 1024, got.shape[2]), bf16),
        in_specs=[SMEM, VMEM],
        out_specs=VMEM,
        scratch_shapes=[
            pltpu.VMEM((GROUPS * CAP, got.shape[2]), f32),
            pltpu.VMEM((1024, got.shape[2]), f32),
        ],
        compiler_params=params(),
        name="put_in_place",
    )(place, got)


class Ring:
    def __init__(self, w, base, out, first, send, recv, fsend, frecv):
        g, t = lax.axis_index("grp"), lax.axis_index("tp")
        core = lax.rem(g, 2)
        self.sibling = {"grp": g + 1 - 2 * core}
        z, x = t // 4, lax.rem(t, 4)
        right, left = lax.rem(x + 1, 4), lax.rem(x + 3, 4)
        far = lax.rem(x + 2, 4)
        self.fsend, self.frecv, self.out = fsend, frecv, out
        self.half = pl.ds(pl.multiple_of(first + core * 512, 512), 512)
        src = w.at[pl.ds(pl.multiple_of(base + core * 512, 512), 512)]
        dst = out.at[x, self.half]
        to_right, to_left = {"tp": z * 4 + right}, {"tp": z * 4 + left}
        self.near = [
            remote(src, dst, send.at[0], recv.at[0], to_right),
            remote(src, dst, send.at[1], recv.at[1], to_left),
        ]
        onward = lax.rem(x + 1 + 2 * core, 4)
        behind = lax.rem(x + 3 + 2 * core, 4)
        self.first_in = remote(src, out.at[behind, self.half], send.at[0], recv.at[core], to_right)
        self.second_in = remote(src, out.at[onward, self.half], send.at[0], recv.at[1 - core], to_right)
        moved = out.at[behind, self.half]
        self.relay = remote(moved, moved, send.at[2], recv.at[2], {"tp": z * 4 + onward})
        self.relay_in = remote(
            moved, out.at[far, self.half], send.at[2], recv.at[2], {"tp": z * 4 + onward}
        )
        self.hands = []
        for k, shard in enumerate((behind, onward, far)):
            piece = out.at[shard, self.half]
            self.hands.append(remote(piece, piece, fsend.at[k], frecv.at[k], self.sibling))

    def start(self):
        for copy in self.near:
            copy.start()

    def service(self):
        self.first_in.wait_recv()
        self.relay.start()
        self.hands[0].start()

    def service_more(self):
        self.second_in.wait_recv()
        self.hands[1].start()

    def service_last(self):
        self.relay_in.wait_recv()
        self.hands[2].start()

    def finish(self):
        for copy in self.near:
            copy.wait_send()
        self.relay.wait_send()
        for copy in self.hands:
            copy.wait()


def head_rows(row):
    rows = lax.broadcasted_iota(jnp.int32, (8, 2 * HD), 0)
    lanes = lax.broadcasted_iota(jnp.int32, (8, 2 * HD), 1)
    return jnp.where(lanes // HD == rows, jnp.broadcast_to(row, (8, 2 * HD)), 0.0)


def head_pick(full):
    rows = lax.broadcasted_iota(jnp.int32, (8, 2 * HD), 0)
    lanes = lax.broadcasted_iota(jnp.int32, (8, 2 * HD), 1)
    return jnp.sum(jnp.where(lanes // HD == rows, full, 0.0), axis=0, keepdims=True)


def dot(a, b):
    return jnp.dot(a, b, preferred_element_type=f32)


def dot_t(a, b):
    return lax.dot_general(a, b, (((1,), (1,)), ((), ())), preferred_element_type=f32)


def self_kernel(
    rows, fresh, prefix, cached, w_self, hidden, gain, w_query, w,
    got, gathered, delta, query,
    vc, vs, vq, attended, part, red, full,
    lsem, ysend, yrecv, psend, precv, asend, arecv, wsend, wrecv, fsend, frecv,
):
    g, t = lax.axis_index("grp"), lax.axis_index("tp")
    x = lax.rem(t, 4)
    loads = [
        pltpu.make_async_copy(cached, vc, lsem.at[0]),
        pltpu.make_async_copy(w_self, vs, lsem.at[1]),
        pltpu.make_async_copy(w_query, vq, lsem.at[2]),
        pltpu.make_async_copy(rows.at[g], got.at[g], lsem.at[3]),
        pltpu.make_async_copy(w.at[pl.ds(0, 1024)], gathered.at[x], lsem.at[4]),
    ]
    for copy in loads:
        copy.start()
    groups = [lax.rem(g + d, GROUPS) for d in range(1, GROUPS)]
    lanes = [lax.rem(t + d, LANES) for d in range(1, LANES)]
    greet([{"grp": p} for p in groups] + [{"tp": p} for p in lanes])
    ring = Ring(w, 0, gathered, 0, wsend, wrecv, fsend, frecv)
    sends = []
    for k, p in enumerate(groups):
        copy = remote(rows.at[p], got.at[g], ysend.at[k], yrecv.at[k], {"grp": p})
        copy.start()
        sends.append(copy)
    ring.start()

    loads[0].wait()
    positions = lax.broadcasted_iota(jnp.int32, (8, CACHE), 1)
    for b in range(8):
        spread = head_rows(fresh[0, pl.ds(b, 1), :])
        scores = dot_t(spread.astype(bf16), vc[b, 0]) * ROOT
        fresh_score = jnp.sum(spread * fresh[1, pl.ds(b, 1), :], axis=1, keepdims=True) * ROOT
        live = positions < prefix[b]
        top = jnp.maximum(
            jnp.max(jnp.where(live, scores, -jnp.inf), axis=1, keepdims=True), fresh_score
        )
        raised = jnp.where(live, jnp.exp(scores - top), 0.0)
        fresh_raised = jnp.exp(fresh_score - top)
        total = jnp.sum(raised, axis=1, keepdims=True) + fresh_raised
        weights = (raised / total).astype(bf16)
        fresh_weight = (fresh_raised / total).astype(bf16).astype(f32)
        mixed = dot(weights, vc[b, 1]) + fresh_weight * fresh[2, pl.ds(b, 1), :]
        attended[pl.ds(b, 1), :] = head_pick(mixed)
    ring.service()
    loads[1].wait()
    held = attended[...].astype(bf16)
    reduce = []
    for d in range(1, LANES + 1):
        p = lax.rem(t + d, LANES)
        part[p] = dot(held, vs[:, pl.ds(pl.multiple_of(p * 512, 512), 512)])
        if d < LANES:
            copy = remote(part.at[p], red.at[t], psend.at[d - 1], precv.at[d - 1], {"tp": p})
            copy.start()
            reduce.append(copy)
    ring.service_more()
    total = part[t]
    for d, copy in enumerate(reduce):
        copy.wait_recv()
        total = total + red[lax.rem(t + LANES - 1 - d, LANES)]
    full[t] = total
    share = []
    for d, p in enumerate(lanes):
        copy = remote(full.at[t], full.at[t], asend.at[d], arecv.at[d], {"tp": p})
        copy.start()
        share.append(copy)
    ring.service_last()
    for d, copy in enumerate(share):
        copy.wait_recv()
    squares = jnp.zeros((8, 512), f32)
    for c in range(LANES):
        at = pl.ds(c * 512, 512)
        summed = full[c]
        delta[:, at] = summed.astype(bf16)
        r = hidden[:, at].astype(f32) + summed
        squares = squares + r * r
    scale = lax.rsqrt(jnp.sum(squares, axis=1, keepdims=True) / (LANES * 512) + epsilon)
    loads[2].wait()
    out = jnp.zeros((8, 2 * HD), f32)
    for c in range(LANES):
        at = pl.ds(c * 512, 512)
        r = hidden[:, at].astype(f32) + full[c]
        normed = (r * scale * gain[:, at]).astype(bf16)
        out = out + dot(normed, vq[at, :])
    query[...] = out.astype(bf16).astype(f32)
    for copy in reduce:
        copy.wait_send()
    for copy in share:
        copy.wait_send()
    for copy in sends:
        copy.wait()
    ring.finish()
    loads[3].wait()
    loads[4].wait()


def self_part(rows, fresh, prefix, cached, w_self, hidden, gain, w_query, w):
    return pl.pallas_call(
        self_kernel,
        out_shape=(
            jax.ShapeDtypeStruct(rows.shape, bf16),
            jax.ShapeDtypeStruct((4, 1024, 512), bf16),
            jax.ShapeDtypeStruct(hidden.shape, bf16),
            jax.ShapeDtypeStruct((8, 2 * HD), f32),
        ),
        in_specs=[ANY, VMEM, SMEM, ANY, ANY, VMEM, VMEM, ANY, ANY],
        out_specs=(ANY, ANY, VMEM, VMEM),
        scratch_shapes=[
            pltpu.VMEM(cached.shape, bf16),
            pltpu.VMEM(w_self.shape, bf16),
            pltpu.VMEM(w_query.shape, bf16),
            pltpu.VMEM((8, 2 * HD), f32),
            pltpu.VMEM((LANES, 8, 512), f32),
            pltpu.VMEM((LANES, 8, 512), f32),
            pltpu.VMEM((LANES, 8, 512), f32),
            DMA((5,)),
            DMA((7,)),
            DMA((7,)),
            DMA((15,)),
            DMA((15,)),
            DMA((15,)),
            DMA((15,)),
            DMA((3,)),
            DMA((3,)),
            DMA((3,)),
            DMA((3,)),
        ],
        compiler_params=params(0),
        name="self_part",
    )(rows, fresh, prefix, cached, w_self, hidden, gain, w_query, w)


def cross_kernel(
    rows, query, beams, slots, counts, gain, gathered, w, w_cross,
    delta,
    zb, vw, vx, enc, pairs, qb, asent, ab, part, red, full,
    lsem, xsend, xrecv, zsend, zrecv, qsend, qrecv, bsend, brecv,
    psend, precv, gsend, grecv, wsend, wrecv, fsend, frecv,
):
    g, t = lax.axis_index("grp"), lax.axis_index("tp")
    z, x = t // 4, lax.rem(t, 4)
    loads = [
        pltpu.make_async_copy(gathered, vw.at[:, pl.ds(0, 1024)], lsem.at[0]),
        pltpu.make_async_copy(w.at[pl.ds(1024, 1024)], vw.at[x, pl.ds(1024, 1024)], lsem.at[1]),
        pltpu.make_async_copy(w_cross, vx, lsem.at[2]),
        pltpu.make_async_copy(query, qb.at[g, x], lsem.at[3]),
    ]
    own = [
        pltpu.make_async_copy(
            rows.at[x, pl.ds(c * 256, 256)], zb.at[z, c, x], lsem.at[4 + c]
        )
        for c in range(4)
    ]
    for copy in loads + own:
        copy.start()
    lanes = [lax.rem(t + d, LANES) for d in range(1, LANES)]
    cloud = []
    for dg in range(GROUPS):
        for dx in range(4):
            if dg or dx:
                cloud.append((lax.rem(g + dg, GROUPS), lax.rem(x + dx, 4), dg, dx))
    greet(
        [{"tp": p} for p in lanes]
        + [{"grp": pg, "tp": z * 4 + px} for pg, px, dg, _ in cloud if dg]
    )
    ring = Ring(w, 1024, vw, 1024, wsend, wrecv, fsend, frecv)
    xs = []
    for c in range(4):
        line = []
        for d in range(1, 4):
            px = lax.rem(x + d, 4)
            copy = remote(
                rows.at[px, pl.ds(c * 256, 256)], zb.at[z, c, x],
                xsend.at[c, d - 1], xrecv.at[c, d - 1], {"tp": z * 4 + px},
            )
            copy.start()
            line.append(copy)
        xs.append(line)
    ring.start()
    asks = []
    for k, (pg, px, dg, dx) in enumerate(cloud):
        copy = remote(
            query, qb.at[g, x], qsend.at[k], qrecv.at[k], {"grp": pg, "tp": z * 4 + px}
        )
        copy.start()
        asks.append(copy)
    up, down = lax.rem(z + 1, 4), lax.rem(z + 3, 4)
    ups, downs, relays = [], [], []
    for c in range(4):
        own[c].wait()
        for copy in xs[c]:
            copy.wait_recv()
        mine = zb.at[z, c]
        ups.append(remote(mine, mine, zsend.at[c, 0], zrecv.at[c, 0], {"tp": up * 4 + x}))
        downs.append(remote(mine, mine, zsend.at[c, 1], zrecv.at[c, 1], {"tp": down * 4 + x}))
        ups[c].start()
        downs[c].start()
    ring.service()
    for c in range(4):
        if c % 2 == 0:
            ups[c].wait_recv()
            piece, to = zb.at[down, c], up
        else:
            downs[c].wait_recv()
            piece, to = zb.at[up, c], down
        relays.append(remote(piece, piece, zsend.at[c, 2], zrecv.at[c, 2], {"tp": to * 4 + x}))
        relays[c].start()
        if c == 0:
            ring.service_more()
        if c == 1:
            ring.service_last()
    for copy in loads:
        copy.wait()
    ring.finish()
    for copy in asks:
        copy.wait()
    for c in range(4):
        if c % 2 == 0:
            downs[c].wait_recv()
        else:
            ups[c].wait_recv()
        relays[c].wait_recv()
        squares = jnp.zeros((256, HD), f32)
        for p in range(LANES):
            piece = zb[p // 4, c, p % 4].astype(f32)
            squares = squares + piece * piece
        scale = lax.rsqrt(jnp.sum(squares, axis=1, keepdims=True) / DE + epsilon)
        for p in range(LANES):
            at = pl.ds(p * HD, HD)
            enc[:, at] = (zb[p // 4, c, p % 4].astype(f32) * scale * gain[:, at]).astype(bf16)

        def project(k, carry):
            pairs[c, k] = dot(enc[...], vw[k]).astype(bf16)
            return carry

        lax.fori_loop(0, 4, project, 0)

    first = g * 8 + x * 2
    numbers = lax.broadcasted_iota(jnp.int32, (8, 64), 0) + first
    chosen = (numbers == beams[...]).astype(bf16)
    tokens = lax.broadcasted_iota(jnp.int32, (8, KMAX * NLEN), 1)
    sides = lax.broadcasted_iota(jnp.int32, (8, 2 * HD), 0)
    for k in range(4):
        asked = dot(chosen, qb[:, k].reshape(64, 2 * HD).astype(bf16))
        answers = []
        for i in range(2):
            spread = head_rows(asked[i : i + 1, :]).astype(bf16)
            scores = jnp.concatenate(
                [dot_t(spread, pairs[2 * i + h, k, :, : 2 * HD]) for h in range(2)], axis=1
            )
            live = tokens < counts[first + i] * NLEN
            scores = jnp.where(live, scores * ROOT, -jnp.inf)
            raised = jnp.exp(scores - jnp.max(scores, axis=1, keepdims=True))
            weights = (raised / jnp.sum(raised, axis=1, keepdims=True)).astype(bf16)
            mixed = dot(weights[:, :256], pairs[2 * i, k, :, 2 * HD :])
            mixed = mixed + dot(weights[:, 256:], pairs[2 * i + 1, k, :, 2 * HD :])
            answers.append(head_pick(mixed))
        asent[k] = jnp.where(
            sides == 0, answers[0], jnp.where(sides == 1, answers[1], 0.0)
        ).astype(bf16).astype(f32)
    ab[g, x] = asent[x]
    replies = []
    for k, (pg, px, dg, dx) in enumerate(cloud):
        copy = remote(
            asent.at[px], ab.at[g, x], bsend.at[k], brecv.at[k], {"grp": pg, "tp": z * 4 + px}
        )
        copy.start()
        replies.append(copy)
    for copy in replies:
        copy.wait_recv()
    spots = lax.broadcasted_iota(jnp.int32, (8, 256), 1)
    inner = lax.rem(spots, 8)
    owner = (spots // 32) * 8 + lax.rem(spots // 8, 4) * 2 + inner
    picks = ((owner == slots[...]) & (inner < 2)).astype(bf16)
    held = dot(picks, ab[...].reshape(256, 2 * HD).astype(bf16)).astype(bf16)
    reduce = []
    for d in range(1, LANES + 1):
        p = lax.rem(t + d, LANES)
        part[p] = dot(held, vx[:, pl.ds(pl.multiple_of(p * 512, 512), 512)])
        if d < LANES:
            copy = remote(part.at[p], red.at[t], psend.at[d - 1], precv.at[d - 1], {"tp": p})
            copy.start()
            reduce.append(copy)
    total = part[t]
    for d, copy in enumerate(reduce):
        copy.wait_recv()
        total = total + red[lax.rem(t + LANES - 1 - d, LANES)]
    full[t] = total
    share = []
    for d, p in enumerate(lanes):
        copy = remote(full.at[t], full.at[t], gsend.at[d], grecv.at[d], {"tp": p})
        copy.start()
        share.append(copy)
    for copy in share:
        copy.wait_recv()
    for c in range(LANES):
        delta[:, pl.ds(c * 512, 512)] = full[c].astype(bf16)
    for line in xs:
        for copy in line:
            copy.wait_send()
    for copy in ups + downs + relays + replies + reduce + share:
        copy.wait_send()


def cross_part(rows, query, beams, slots, counts, gain, gathered, w, w_cross, width):
    return pl.pallas_call(
        cross_kernel,
        out_shape=jax.ShapeDtypeStruct((8, width), bf16),
        in_specs=[ANY, VMEM, VMEM, VMEM, SMEM, VMEM, ANY, ANY, ANY],
        out_specs=VMEM,
        scratch_shapes=[
            pltpu.VMEM((4, 4, 4, 256, HD), bf16),
            pltpu.VMEM((4, DE, 512), bf16),
            pltpu.VMEM(w_cross.shape, bf16),
            pltpu.VMEM((256, DE), bf16),
            pltpu.VMEM((4, 4, 256, 512), bf16),
            pltpu.VMEM((GROUPS, 4, 8, 2 * HD), f32),
            pltpu.VMEM((4, 8, 2 * HD), f32),
            pltpu.VMEM((GROUPS, 4, 8, 2 * HD), f32),
            pltpu.VMEM((LANES, 8, 512), f32),
            pltpu.VMEM((LANES, 8, 512), f32),
            pltpu.VMEM((LANES, 8, 512), f32),
            DMA((8,)),
            DMA((4, 3)),
            DMA((4, 3)),
            DMA((4, 3)),
            DMA((4, 3)),
            DMA((31,)),
            DMA((31,)),
            DMA((31,)),
            DMA((31,)),
            DMA((15,)),
            DMA((15,)),
            DMA((15,)),
            DMA((15,)),
            DMA((3,)),
            DMA((3,)),
            DMA((3,)),
            DMA((3,)),
        ],
        compiler_params=params(1),
        name="cross_part",
    )(rows, query, beams, slots, counts, gain, gathered, w, w_cross)


def local(
    neighbour_ids,
    neighbour_shard,
    neighbour_count,
    slot_beam,
    prefix_length,
    embed_table,
    encoder_gain,
    hidden_in,
    decoder_gain,
    fresh_projections,
    cached_pairs,
    w_self_out,
    w_query,
    w_pairs,
    w_cross_out,
):
    me = lax.axis_index("grp")
    shards = neighbour_shard.reshape(neighbour_ids.shape)
    wanted, filled, place = prepare(neighbour_ids, shards, neighbour_count, me)
    rows = look(wanted, filled, embed_table)
    w = w_pairs.reshape(DE, 512)
    fresh = jnp.transpose(fresh_projections.astype(f32), (1, 0, 2))
    got, gathered, self_delta, query = self_part(
        rows, fresh, prefix_length, cached_pairs, w_self_out, hidden_in,
        decoder_gain[None, :], w_query, w,
    )
    placed = put_in_place(place, got)
    slots = lax.dynamic_slice_in_dim(slot_beam, me * 8, 8)
    cross_delta = cross_part(
        placed, query, slot_beam[None, :], slots[:, None], neighbour_count,
        encoder_gain[None, :], gathered, w, w_cross_out, hidden_in.shape[1],
    )
    return self_delta, cross_delta


def solution(mesh):
    placed = (
        P(),
        P(),
        P(),
        P(),
        P("grp"),
        P("grp", "tp"),
        P(),
        P("grp", None),
        P(),
        P("grp", None, "tp"),
        P("grp", None, None, "tp"),
        P("tp", None),
        P(None, "tp"),
        P(None, None, "tp"),
        P("tp", None),
    )
    return jax.shard_map(
        local,
        mesh=mesh,
        in_specs=placed,
        out_specs=(P("grp", None), P("grp", None)),
        check_vma=False,
    )
```

time: 600 us -> 169 us (0.28)
  waiting for transfers between devices: 240 us -> 0 us
  blocking collectives: 149 us -> 0 us
  Pallas kernels: 0 us -> 143 us
  local copies, waits for them, and re-layouts: 143 us -> 9.4 us
  matrix products: 23 us -> 3.29 us
  other arithmetic: 27 us -> 11.8 us
  between operations: 15.7 us -> 0.79 us
    psum x2 -> x0, blocking collectives: 149 us -> none  [the longest x1 75 us: local(): lax.psum(jnp.dot(cross_attended, w_cross_out, preferred_element_type=jnp....]
    all_gather x2 -> x0, waiting for transfers between devices: 145 us -> none  [the longest x1 117 us: local(): lax.all_gather(flat_rows, 'tp', axis=1, tiled=True)]
    pallas_call x0 -> x4, Pallas kernels: none -> 143 us  [the longest x1 85.2 us: cross_part(): pl.pallas_call(cross_kernel, out_shape=jax.ShapeDtypeStruct((8, width), b...]
    gather x2 -> x0, local copies, waits for them, and re-layouts: 116 us -> none  [the longest x1 112 us: dense_rows(): looked = jnp.take(embed_table, offset_ids.reshape(-1), axis=0)]
    reduce_scatter x1 -> x0, waiting for transfers between devices: 54.2 us -> none  [local(): lax.psum_scatter(partial_rows, 'grp', scatter_dimension=0, tiled=True)]
    psum x1 -> x0, waiting for transfers between devices: 41.1 us -> none  [local(): lax.psum(jnp.dot(attended, w_self_out, preferred_element_type=jnp.float32...]
    dot_general x8 -> x5, matrix products: 23 us -> 3.29 us  [the longest x1 2.59 us: prepare(): jnp.einsum('gra,grb->gab', first, parts.reshape(GROUPS, rows, 64), prefer...]
    select_n x4 -> x1, other arithmetic: 17.2 us -> 0.12 us  [prepare(): ids3 // 128]
  transfers between devices with their start and end apart: 4 -> 0, of which waited for: 4 -> 0; matrix products, arithmetic and copies ran while one was open for 5% -> 0% of each run, Pallas kernels for 0% -> 0%
where the time goes in v1:
time: 169 us; the launch traced here: 168 us
  Pallas kernels  143 us (85%)
  other arithmetic  11.8 us (7%)
  local copies, waits for them, and re-layouts  9.4 us (6%)
  matrix products  3.29 us (2%)
    pallas_call x1, Pallas kernels, cross_part(): pl.pallas_call(cross_kernel, out_shape=jax.ShapeDtypeStruct((8, width), b...  85.2 us
    pallas_call x1, Pallas kernels, self_part(): pl.pallas_call(self_kernel, out_shape=(jax.ShapeDtypeStruct(rows.shape, b...  44.9 us
    pallas_call x1, Pallas kernels, put_in_place(): pl.pallas_call(place_kernel, out_shape=jax.ShapeDtypeStruct((4, 1024, got...  7.43 us
    reduce_sum x2, other arithmetic, prepare(): filled = jnp.sum(mine.astype(jnp.int32), axis=(1, 2))  7.31 us
    pallas_call x1, Pallas kernels, look(): pl.pallas_call(look_kernel, out_shape=jax.ShapeDtypeStruct((GROUPS, CAP,...  5.64 us
    unnamed x16, local copies, waits for them, and re-layouts  4.21 us

profile of v1, /device:TPU:0, one launch (start us, length us, event | category | flops | bytes accessed | tf_op | source)
XLA Modules:
  0.0 168.4 jit_solution(6909671483264273992)
XLA Ops:
  0.6 0.7 broadcast_in_dim.69
  1.7 6.7 %fusion.11 = (s32[256]{0:T(256)S(1)}, pred[256,128,1]{1,2,0:T(4,128)(4,1)S(1)}) fusion(pred[256]{0:T(512)(128)(4,1)S(1)} %fusion.46, s32[256,128,1]{1,2,0:T(1,128)} %param.16, s32[]{:T(128)S(6)} %axis_index.15), kind=kLoop, calls=%fused_computation.36 | loop fusion | flops 130816 | bytes 165124 | tf_op jit(solution)/shard_map/reduce_sum | solution.py:82
  8.6 0.2 fusion.17
  8.9 0.2 fusion.21
  9.2 0.2 fusion.8
  9.6 0.9 reshape.150
  10.6 2.3 %select_convert_fusion.1 = (bf16[8,4096,32]{1,2,0:T(8,128)(2,1)S(1)}, bf16[8,4096,32]{1,2,0:T(8,128)(2,1)}) fusion(s32[8,4096]{1,0:T(8,128)S(1)} %get-tuple-element.16, s32[8,4096]{1,0:T(8,128)S(1)} %get-tuple-element.18, s32[8,4096]{1,0:T(8,128)S(1)} %get-tuple-element.17), kind=kLoop, calls=%fused_computation.5 | loop fusion | flops 5242880 | bytes 4587520 | tf_op jit(solution)/shard_map/convert.2
  12.9 0.4 reduce.3
  13.4 2.6 %fusion = f32[8,32,64]{2,1,0:T(8,128)S(1)} fusion(bf16[8,4096,32]{1,2,0:T(8,128)(2,1)} %get-tuple-element.15, bf16[8,4096,32]{1,2,0:T(8,128)(2,1)S(1)} %get-tuple-element.14, s32[8,4096]{1,0:T(8,128)S(1)} %get-tuple-element.19, pred[8,4096]{1,0:T(8,128)(4,1)S(1)} %bitcast_and_fusion), kind=kOutput, calls=%fused_computation | convolution fusion | flops 144703488 | bytes 4423680 | tf_op jit(solution)/shard_map/gra,grb->gab/dot_general | solution.py:78
  16.1 0.7 reshape.151.wanted
  16.9 0.6 reduce_sum.27.filled
  17.6 5.6 %look.1.rows = bf16[8,1024,128]{2,1,0:T(8,128)(2,1)} custom-call(s32[8192]{0:T(1024)} %reshape.151.wanted, s32[8]{0:T(128)} %reduce_sum.27.filled, bf16[16000,128]{1,0:T(8,128)(2,1)} %table.1), custom_call_target="tpu_custom_call" | custom-call | tf_op jit(solution)/shard_map/look/pallas_call | solution.py:117
  23.2 1.8 %copy.34 = bf16[256,8,2,256]{3,1,2,0:T(8,128)(2,1)} copy(bf16[256,8,2,256]{3,2,1,0:T(2,128)(2,1)S(1)} %bitcast.33) | data formatting | bytes 4194304
  25.0 0.6 convert_bitcast_fusion.fresh
  25.6 44.9 %self_part.1 = (bf16[8,1024,128]{2,1,0:T(8,128)(2,1)}, bf16[4,1024,512]{2,1,0:T(8,128)(2,1)}, bf16[8,8192]{1,0:T(8,128)(2,1)}, f32[8,256]{1,0:T(8,128)}) custom-call(bf16[8,1024,128]{2,1,0:T(8,128)(2,1)} %look.1.rows, f32[3,8,256]{2,1,0:T(8,128)} %convert_bitcast_fusion.fresh, s32[8]{0:T(128)} %prefix.1, bf16[8,2,512,256]{3,2,1,0:T(8,128)(2,1)} %cached.1, ...), custom_call_target="tpu_custom_call" | custom-call | tf_op jit(solution)/shard_map/self_part/pallas_call | solution.py:336
  70.8 0.7 constant_dynamic-slice_fusion
  71.5 0.2 fusion.15
  71.7 0.2 fusion.22
  72.1 0.7 select_reduce_fusion
  72.8 7.4 %put_in_place.1.rows = bf16[4,1024,128]{2,1,0:T(8,128)(2,1)} custom-call(s32[4096]{0:T(1024)} %bitcast.37, bf16[8,1024,128]{2,1,0:T(8,128)(2,1)} %get-tuple-element.7.got), custom_call_target="tpu_custom_call" | custom-call | tf_op jit(solution)/shard_map/put_in_place/pallas_call | solution.py:148
  80.3 0.7 copy.28.slots
  81.0 85.2 %cross_part.1 = bf16[8,8192]{1,0:T(8,128)(2,1)} custom-call(bf16[4,1024,128]{2,1,0:T(8,128)(2,1)} %put_in_place.1.rows, f32[8,256]{1,0:T(8,128)} %get-tuple-element.8.query, s32[1,64]{1,0:T(1,128)} %bitcast.41, s32[8,1]{1,0:T(8,128)} %copy.28.slots, s32[64]{0:T(128)} %counts.1, f32[1,2048]{1,0:T(1,128)} %bitcast.40, ...), custom_call_target="tpu_custom_call" | custom-call | tf_op jit(solution)/shard_map/cross_part/pallas_call | solution.py:544
  166.2 0.7 copy.41
  166.8 1.6 copy.42
  (37 shorter events, 1.8 us)
Async XLA Ops:
  16.0 7.2 %copy-start = (bf16[2048,2,256]{2,1,0:T(2,128)(2,1)S(1)}, bf16[2048,2,256]{2,1,0:T(2,128)(2,1)}, u32[]{:S(2)}) copy-start(bf16[2048,2,256]{2,1,0:T(2,128)(2,1)} %param.28) | copy-start | bytes 6291460
  17.6 7.4 %copy-start.2 = (bf16[8,3,256]{2,0,1:T(8,128)(2,1)S(1)}, bf16[8,3,256]{2,0,1:T(8,128)(2,1)}, u32[]{:S(2)}) copy-start(bf16[8,3,256]{2,0,1:T(8,128)(2,1)} %param.24) | copy-start | bytes 36868
  25.6 44.9 %copy-start.3 = (s32[64]{0:T(128)S(1)}, s32[64]{0:T(128)}, u32[]{:S(2)}) copy-start(s32[64]{0:T(128)} %counts.1) | copy-start | bytes 772
  25.6 54.6 %copy-start.4 = (s32[64]{0:T(128)S(1)}, s32[64]{0:T(128)}, u32[]{:S(2)}) copy-start(s32[64]{0:T(128)} %param.18) | copy-start | bytes 772
  81.0 85.2 %copy-start.1 = (bf16[8,8192]{1,0:T(8,128)(2,1)S(1)}, bf16[8,8192]{1,0:T(8,128)(2,1)}, u32[]{:S(2)}) copy-start(bf16[8,8192]{1,0:T(8,128)(2,1)} %get-tuple-element.22) | copy-start | bytes 393220

commit v2 on v0

v2 whole, which is shorter than its diff:
```python
import math

import jax
import jax.numpy as jnp
from jax import lax
from jax.experimental import pallas as pl
from jax.experimental.pallas import tpu as pltpu
from jax.sharding import PartitionSpec as P

MESH = pl.DeviceIdType.MESH
DMA = pltpu.SemaphoreType.DMA
VMEM = pl.BlockSpec(memory_space=pltpu.VMEM)
SMEM = pl.BlockSpec(memory_space=pltpu.SMEM)
ANY = pl.BlockSpec(memory_space=pl.ANY)

HD = 128
DE = 2048
NLEN = 128
KMAX = 4
CACHE = 512
CAP = 1024
GROUPS = 8
LANES = 16
ROOT = 1.0 / math.sqrt(HD)
epsilon = 1e-05
f32 = jnp.float32
bf16 = jnp.bfloat16
BIG = 62 * 2**20


def params(cid=None):
    if cid is None:
        return pltpu.CompilerParams(vmem_limit_bytes=BIG)
    return pltpu.CompilerParams(collective_id=cid, has_side_effects=True, vmem_limit_bytes=BIG)


def remote(src, dst, send, recv, where):
    return pltpu.make_async_remote_copy(
        src_ref=src, dst_ref=dst, send_sem=send, recv_sem=recv, device_id=where, device_id_type=MESH
    )


def head_rows(row):
    rows = lax.broadcasted_iota(jnp.int32, (8, 2 * HD), 0)
    lanes = lax.broadcasted_iota(jnp.int32, (8, 2 * HD), 1)
    return jnp.where(lanes // HD == rows, jnp.broadcast_to(row, (8, 2 * HD)), 0.0)


def head_pick(full):
    rows = lax.broadcasted_iota(jnp.int32, (8, 2 * HD), 0)
    lanes = lax.broadcasted_iota(jnp.int32, (8, 2 * HD), 1)
    return jnp.sum(jnp.where(lanes // HD == rows, full, 0.0), axis=0, keepdims=True)


def dot(a, b):
    return jnp.dot(a, b, preferred_element_type=f32)


def dot_t(a, b):
    return lax.dot_general(a, b, (((1,), (1,)), ((), ())), preferred_element_type=f32)


def prep_kernel(ids, shards, counts, wanted, place):
    me = lax.axis_index("grp")
    rows = lax.broadcasted_iota(jnp.int32, (256, 1), 0)
    of_beam = (
        lax.broadcasted_iota(jnp.int32, (256, 64), 0) // KMAX
        == lax.broadcasted_iota(jnp.int32, (256, 64), 1)
    ).astype(bf16)
    held = dot(of_beam, jnp.broadcast_to(counts[...], (64, NLEN)).astype(bf16))
    alive = (rows % KMAX).astype(f32) < held
    upper = (
        lax.broadcasted_iota(jnp.int32, (NLEN, NLEN), 0)
        <= lax.broadcasted_iota(jnp.int32, (NLEN, NLEN), 1)
    ).astype(bf16)
    down = lax.broadcasted_iota(jnp.int32, (256, 256), 0)
    along = lax.broadcasted_iota(jnp.int32, (256, 256), 1)
    before = ((down // 32 == along // 32) & (along < down)).astype(bf16)
    ones = jnp.ones((NLEN, NLEN), bf16)

    def ranks(mask):
        mask = mask.astype(bf16)
        return dot(mask, upper) + dot(before, dot(mask, ones).astype(bf16)) - 1.0

    mine = (shards[...] == me) & alive
    rank = jnp.where(mine, ranks(mine), -1.0).astype(jnp.int32)
    high, low = rank >> 5, rank & 31
    high = jnp.where(mine, high, -1)
    id_high, id_low = (ids[...] >> 7).astype(f32), (ids[...] & 127).astype(f32)
    small = lax.broadcasted_iota(jnp.int32, (32, NLEN), 0)
    for g in range(GROUPS):
        left, right = [], []
        for i in range(32 * g, 32 * g + 32):
            left.append((small == high[i : i + 1]).astype(bf16))
            spot = small == low[i : i + 1]
            right.append(
                jnp.concatenate(
                    [
                        jnp.where(spot, id_high[i : i + 1], 0.0).astype(bf16),
                        jnp.where(spot, id_low[i : i + 1], 0.0).astype(bf16),
                    ],
                    axis=0,
                )
            )
        both = dot_t(jnp.concatenate(left, axis=1), jnp.concatenate(right, axis=1))
        wanted[g] = (both[:, :32] * 128.0 + both[:, 32:]).astype(jnp.int32)

    at = pl.ds(pl.multiple_of(me * 32, 32), 32)
    own = jnp.concatenate([shards[at, :]] * GROUPS, axis=0)
    beam = me * 8 + lax.broadcasted_iota(jnp.int32, (256, 64), 0) % 32 // KMAX
    of_own = (beam == lax.broadcasted_iota(jnp.int32, (256, 64), 1)).astype(bf16)
    own_held = dot(of_own, jnp.broadcast_to(counts[...], (64, NLEN)).astype(bf16))
    named = (own == rows // 32) & ((rows % KMAX).astype(f32) < own_held)
    spots = jnp.where(named, ranks(named) + (rows // 32 * CAP).astype(f32), 0.0).astype(jnp.int32)
    total = spots[0:32]
    for s in range(1, GROUPS):
        total = total + spots[32 * s : 32 * s + 32]
    place[...] = total


def prepare(ids, shards, counts):
    return pl.pallas_call(
        prep_kernel,
        out_shape=(
            jax.ShapeDtypeStruct((GROUPS, 32, 32), jnp.int32),
            jax.ShapeDtypeStruct((32, NLEN), jnp.int32),
        ),
        in_specs=[VMEM, VMEM, VMEM],
        out_specs=(VMEM, VMEM),
        compiler_params=params(),
        name="prep",
    )(ids, shards, counts)


class Ring:
    def __init__(self, out, here, peer, sems):
        g = lax.axis_index("grp")
        core = lax.rem(g, 2)
        send, recv, fsend, frecv = sems
        half = pl.ds(pl.multiple_of(core * 1024, 1024), 1024)
        right, left = lax.rem(here + 1, 4), lax.rem(here + 3, 4)
        onward, behind = lax.rem(here + 1 + 2 * core, 4), lax.rem(here + 3 + 2 * core, 4)
        mine, moved = out.at[here, half], out.at[behind, half]
        self.near = [
            remote(mine, mine, send.at[0], recv.at[0], peer(right)),
            remote(mine, mine, send.at[1], recv.at[1], peer(left)),
        ]
        self.first_in = remote(mine, moved, send.at[0], recv.at[core], peer(right))
        self.second_in = remote(
            mine, out.at[onward, half], send.at[0], recv.at[1 - core], peer(right)
        )
        self.relay = remote(moved, moved, send.at[2], recv.at[2], peer(onward))
        self.relay_in = remote(
            moved, out.at[lax.rem(here + 2, 4), half], send.at[2], recv.at[2], peer(onward)
        )
        self.hands = []
        for k, shard in enumerate((behind, onward, lax.rem(here + 2, 4))):
            piece = out.at[shard, half]
            self.hands.append(
                remote(piece, piece, fsend.at[k], frecv.at[k], {"grp": g + 1 - 2 * core})
            )

    def start(self):
        for copy in self.near:
            copy.start()

    def service(self):
        self.first_in.wait_recv()
        self.relay.start()
        self.hands[0].start()

    def service_more(self):
        self.second_in.wait_recv()
        self.hands[1].start()

    def service_last(self):
        self.relay_in.wait_recv()
        self.hands[2].start()

    def finish(self):
        for copy in self.near:
            copy.wait_send()
        self.relay.wait_send()
        for copy in self.hands:
            copy.wait()


class Spread:
    def __init__(self, held, weights, part, red, full, sems):
        self.held, self.weights, self.part, self.red, self.full = held, weights, part, red, full
        self.psend, self.precv, self.asend, self.arecv = sems
        self.t = lax.axis_index("tp")

    def start(self):
        self.reduce = []
        for d in range(1, LANES + 1):
            p = lax.rem(self.t + d, LANES)
            at = pl.ds(pl.multiple_of(p * 512, 512), 512)
            self.part[p] = dot(self.held, self.weights[:, at])
            if d < LANES:
                copy = remote(
                    self.part.at[p], self.red.at[self.t],
                    self.psend.at[d - 1], self.precv.at[d - 1], {"tp": p},
                )
                copy.start()
                self.reduce.append(copy)

    def share(self):
        total = self.part[self.t]
        for d, copy in enumerate(self.reduce):
            copy.wait_recv()
            total = total + self.red[lax.rem(self.t + LANES - 1 - d, LANES)]
        self.full[self.t] = total
        self.shared = []
        for d in range(1, LANES):
            mine = self.full.at[self.t]
            copy = remote(
                mine, mine, self.asend.at[d - 1], self.arecv.at[d - 1],
                {"tp": lax.rem(self.t + d, LANES)},
            )
            copy.start()
            self.shared.append(copy)

    def arrive(self):
        for copy in self.shared:
            copy.wait_recv()

    def finish(self):
        for copy in self.reduce + self.shared:
            copy.wait_send()


class Move:
    def __init__(self, placed, first, out, a, b, peer_a, peer_b, sems):
        self.asend, self.arecv, self.bsend, self.brecv, self.own = sems
        self.placed, self.first, self.out = placed, first, out
        self.a, self.b, self.peer_a, self.peer_b = a, b, peer_a, peer_b
        self.exchanged, self.ups, self.downs, self.relays, self.kept = {}, {}, {}, {}, {}

    def exchange(self, h):
        a, b = self.a, self.b
        line = []
        for d in (1, 3, 2):
            p = lax.rem(a + d, 4)
            copy = remote(
                self.placed.at[h, self.first + p], self.out.at[b, h, a],
                self.asend.at[h, d - 1], self.arecv.at[h, d - 1], self.peer_a(p),
            )
            copy.start()
            line.append(copy)
        self.exchanged[h] = line
        self.kept[h] = pltpu.make_async_copy(
            self.placed.at[h, self.first + a], self.out.at[b, h, a], self.own.at[h]
        )
        self.kept[h].start()

    def gather(self, h):
        self.kept[h].wait()
        for copy in self.exchanged[h]:
            copy.wait_recv()
        mine = self.out.at[self.b, h]
        up, down = lax.rem(self.b + 1, 4), lax.rem(self.b + 3, 4)
        self.ups[h] = remote(
            mine, mine, self.bsend.at[h, 0], self.brecv.at[h, 0], self.peer_b(up)
        )
        self.downs[h] = remote(
            mine, mine, self.bsend.at[h, 1], self.brecv.at[h, 1], self.peer_b(down)
        )
        self.ups[h].start()
        self.downs[h].start()

    def relay(self, h):
        up, down = lax.rem(self.b + 1, 4), lax.rem(self.b + 3, 4)
        if h % 2 == 0:
            self.ups[h].wait_recv()
            piece, to = self.out.at[down, h], up
        else:
            self.downs[h].wait_recv()
            piece, to = self.out.at[up, h], down
        self.relays[h] = remote(
            piece, piece, self.bsend.at[h, 2], self.brecv.at[h, 2], self.peer_b(to)
        )
        self.relays[h].start()

    def arrive(self, h):
        (self.downs if h % 2 == 0 else self.ups)[h].wait_recv()
        self.relays[h].wait_recv()

    def finish(self):
        for h in self.ups:
            for copy in self.exchanged[h]:
                copy.wait_send()
            for copy in (self.ups[h], self.downs[h], self.relays[h]):
                copy.wait_send()


def step_kernel(
    wanted, place, prefix, counts, fresh, beams, slots, hidden, gain, egain,
    table, cached, w_self, w_query, w, w_cross,
    delta, out,
    tbuf, wide, found, rows, got, wbuf, wx, wz, vc, vs, vq, attended,
    part, red, full, cpart, cred, cfull,
    placed, xb, zb, enc, pairs, qall, qsend_buf, qx, qz, answers, ab, aall,
    tsem, wsem, lsem, ysend, yrecv, rsems, csems, xw, zw, xm, zm,
    qgsend, qgrecv, qtsend, qtrecv, atsend, atrecv, agsend, agrecv,
):
    g, t = lax.axis_index("grp"), lax.axis_index("tp")
    z, x = t // 4, lax.rem(t, 4)
    groups = [lax.rem(g + d, GROUPS) for d in range(1, GROUPS)]
    lanes = [lax.rem(t + d, LANES) for d in range(1, LANES)]
    peers = [{"grp": p} for p in groups] + [{"tp": p} for p in lanes]
    barrier = pltpu.get_barrier_semaphore()
    for peer in peers:
        pl.semaphore_signal(barrier, inc=1, device_id=peer, device_id_type=MESH)

    def by_x(p):
        return {"tp": z * 4 + p}

    def by_z(p):
        return {"tp": p * 4 + x}

    tstep, wstep = table.shape[0] // 10, DE // 8
    tload = [
        pltpu.make_async_copy(
            table.at[pl.ds(i * tstep, tstep)], tbuf.at[i % 2], tsem.at[i % 2]
        )
        for i in range(10)
    ]
    wload = [
        pltpu.make_async_copy(w.at[pl.ds(i * wstep, wstep)], wbuf.at[i % 2], wsem.at[i % 2])
        for i in range(8)
    ]
    for i in range(2):
        tload[i].start()
    for i in range(2):
        wload[i].start()
    loads = [
        pltpu.make_async_copy(cached, vc, lsem.at[0]),
        pltpu.make_async_copy(w_self, vs, lsem.at[1]),
        pltpu.make_async_copy(w_query, vq, lsem.at[2]),
    ]
    for i in range(10):
        tload[i].wait()
        wide[pl.ds(i * tstep, tstep), :] = tbuf[i % 2].astype(f32)
        if i + 2 < 10:
            tload[i + 2].start()
    for copy in loads:
        copy.start()

    def look(p):
        def some(k, c):
            for u in range(32):
                found[k * 32 + u, :] = wide[wanted[p, k, u], :]
            return c

        lax.fori_loop(0, CAP // 32, some, 0)
        return found[...].astype(bf16)

    sends = []

    def look_and_send(d):
        p = groups[d]
        rows[p] = look(p)
        copy = remote(rows.at[p], got.at[g], ysend.at[d], yrecv.at[d], {"grp": p})
        copy.start()
        sends.append(copy)

    rows[groups[0]] = look(groups[0])
    pl.semaphore_wait(barrier, len(peers))
    copy = remote(rows.at[groups[0]], got.at[g], ysend.at[0], yrecv.at[0], {"grp": groups[0]})
    copy.start()
    sends.append(copy)
    look_and_send(1)
    for i in range(8):
        wload[i].wait()
        flat = wbuf[i % 2].reshape(wstep, 512)
        at = pl.ds(i * wstep, wstep)
        wx[x, at, :] = flat
        wz[z, at, :] = flat
        if i + 2 < 8:
            wload[i + 2].start()
    ring_x = Ring(wx, x, by_x, [xw.at[i] for i in range(4)])
    ring_z = Ring(wz, z, by_z, [zw.at[i] for i in range(4)])
    ring_x.start()
    ring_z.start()
    for d in range(2, 7):
        look_and_send(d)
    got[g] = look(g)

    loads[0].wait()
    positions = lax.broadcasted_iota(jnp.int32, (8, CACHE), 1)
    for b in range(8):
        spread = head_rows(fresh[0, pl.ds(b, 1), :])
        scores = dot_t(spread.astype(bf16), vc[b, 0]) * ROOT
        fresh_score = jnp.sum(spread * fresh[1, pl.ds(b, 1), :], axis=1, keepdims=True) * ROOT
        live = positions < prefix[b]
        top = jnp.maximum(
            jnp.max(jnp.where(live, scores, -jnp.inf), axis=1, keepdims=True), fresh_score
        )
        raised = jnp.where(live, jnp.exp(scores - top), 0.0)
        fresh_raised = jnp.exp(fresh_score - top)
        total = jnp.sum(raised, axis=1, keepdims=True) + fresh_raised
        weights = (raised / total).astype(bf16)
        fresh_weight = (fresh_raised / total).astype(bf16).astype(f32)
        mixed = dot(weights, vc[b, 1]) + fresh_weight * fresh[2, pl.ds(b, 1), :]
        attended[pl.ds(b, 1), :] = head_pick(mixed)
    loads[1].wait()
    own_sum = Spread(
        attended[...].astype(bf16), vs, part, red, full, [rsems.at[i] for i in range(4)]
    )
    own_sum.start()
    late = pltpu.make_async_copy(w_cross, vs, lsem.at[3])
    late.start()
    own_sum.share()
    own_sum.arrive()
    squares = jnp.zeros((8, 512), f32)
    for c in range(LANES):
        at = pl.ds(c * 512, 512)
        summed = full[c]
        delta[:, at] = summed.astype(bf16)
        r = hidden[:, at].astype(f32) + summed
        squares = squares + r * r
    scale = lax.rsqrt(jnp.sum(squares, axis=1, keepdims=True) / (LANES * 512) + epsilon)
    loads[2].wait()
    asked = jnp.zeros((8, 2 * HD), f32)
    for c in range(LANES):
        at = pl.ds(c * 512, 512)
        r = hidden[:, at].astype(f32) + full[c]
        normed = (r * scale * gain[:, at]).astype(bf16)
        asked = asked + dot(normed, vq[at, :])
    qall[g] = asked.astype(bf16).astype(f32)
    asks = []
    for d, p in enumerate(groups):
        copy = remote(qall.at[g], qall.at[g], qgsend.at[d], qgrecv.at[d], {"grp": p})
        copy.start()
        asks.append(copy)

    ring_x.service()
    ring_z.service()
    for copy in asks:
        copy.wait_recv()
    numbers = lax.broadcasted_iota(jnp.int32, (8, 64), 0) + g * 8
    chosen = (numbers == beams[...]).astype(bf16)
    routed = dot(chosen, qall[...].reshape(64, 2 * HD).astype(bf16))
    qsend_buf[...] = routed
    qx[x] = routed
    qz[z] = routed
    for d in range(1, 4):
        for k, (to, peer, here) in enumerate(((qx, by_x, x), (qz, by_z, z))):
            copy = remote(
                qsend_buf, to.at[here], qtsend.at[k, d - 1], qtrecv.at[k, d - 1],
                peer(lax.rem(here + d, 4)),
            )
            copy.start()
            asks.append(copy)
    ring_x.service_more()
    ring_z.service_more()

    for copy in sends:
        copy.wait_recv()
    for s in range(GROUPS):
        wide[pl.ds(s * CAP, CAP), :] = got[s].astype(f32)

    def put(h, first):
        def beam(b, c):
            def some(k, c):
                line = (first + b) * 4 + h * 2 + k // 4
                column = lax.rem(k, 4) * 32
                for u in range(32):
                    found[k * 32 + u, :] = wide[place[line, column + u], :]
                return c

            lax.fori_loop(0, 8, some, 0)
            placed[h, first + b] = found[0:256, :].astype(bf16)
            return c

        lax.fori_loop(0, 4, beam, 0)

    move_x = Move(placed, 0, xb, x, z, by_x, by_z, xm)
    move_z = Move(placed, 4, zb, z, x, by_z, by_x, zm)
    for h in range(2):
        put(h, 0)
        move_x.exchange(h)
        put(h, 4)
        move_z.exchange(h)
    ring_x.service_last()
    ring_z.service_last()
    for h in range(2):
        move_x.gather(h)
        move_z.gather(h)
    for h in range(2):
        move_x.relay(h)
        move_z.relay(h)
    ring_x.finish()
    ring_z.finish()

    def encode(h, buf, shards, side, turned):
        def piece(p):
            return buf[p % 4, h, p // 4] if turned else buf[p // 4, h, p % 4]

        squares = jnp.zeros((256, HD), f32)
        for p in range(LANES):
            value = piece(p).astype(f32)
            squares = squares + value * value
        scale = lax.rsqrt(jnp.sum(squares, axis=1, keepdims=True) / DE + epsilon)
        for p in range(LANES):
            at = pl.ds(p * HD, HD)
            enc[:, at] = (piece(p).astype(f32) * scale * egain[:, at]).astype(bf16)

        def project(k, carry):
            pairs[side, h, k] = dot(enc[...], shards[k]).astype(bf16)
            return carry

        lax.fori_loop(0, 4, project, 0)

    tokens = lax.broadcasted_iota(jnp.int32, (8, KMAX * NLEN), 1)

    def attend(side, beam, asked):
        live = tokens < counts[g * 8 + beam] * NLEN
        for k in range(4):
            spread = head_rows(asked[k, pl.ds(beam, 1), :]).astype(bf16)
            scores = jnp.concatenate(
                [dot_t(spread, pairs[side, h, k, :, : 2 * HD]) for h in range(2)], axis=1
            )
            scores = jnp.where(live, scores * ROOT, -jnp.inf)
            raised = jnp.exp(scores - jnp.max(scores, axis=1, keepdims=True))
            weights = (raised / jnp.sum(raised, axis=1, keepdims=True)).astype(bf16)
            mixed = dot(weights[:, :256], pairs[side, 0, k, :, 2 * HD :])
            mixed = mixed + dot(weights[:, 256:], pairs[side, 1, k, :, 2 * HD :])
            answer = head_pick(mixed).astype(bf16).astype(f32)
            answers[side, k] = jnp.broadcast_to(answer, (8, 2 * HD))

    for h in range(2):
        move_x.arrive(h)
        encode(h, xb, wx, 0, False)
        move_z.arrive(h)
        encode(h, zb, wz, 1, True)
    for copy in asks[7:]:
        copy.wait_recv()
    attend(0, x, qx)
    replies = []
    for side, beam, here, peer in ((0, x, x, by_x), (1, 4 + z, z, by_z)):
        if side == 1:
            attend(1, 4 + z, qz)
        for d in range(1, 4):
            p = lax.rem(here + d, 4)
            copy = remote(
                answers.at[side, p], ab.at[side, here],
                atsend.at[side, d - 1], atrecv.at[side, d - 1], peer(p),
            )
            copy.start()
            replies.append(copy)
        ab[side, here] = answers[side, here]
    for copy in replies:
        copy.wait_recv()
    aall[g] = jnp.concatenate(
        [ab[0, k, 0:1] for k in range(4)] + [ab[1, k, 0:1] for k in range(4)], axis=0
    )
    returns = []
    for d, p in enumerate(groups):
        copy = remote(aall.at[g], aall.at[g], agsend.at[d], agrecv.at[d], {"grp": p})
        copy.start()
        returns.append(copy)
    late.wait()
    for copy in returns:
        copy.wait_recv()
    picks = (lax.broadcasted_iota(jnp.int32, (8, 64), 1) == slots[...]).astype(bf16)
    held = dot(picks, aall[...].reshape(64, 2 * HD).astype(bf16)).astype(bf16)
    cross_sum = Spread(held, vs, cpart, cred, cfull, [csems.at[i] for i in range(4)])
    cross_sum.start()
    cross_sum.share()
    cross_sum.arrive()
    for c in range(LANES):
        out[:, pl.ds(c * 512, 512)] = cfull[c].astype(bf16)
    own_sum.finish()
    cross_sum.finish()
    move_x.finish()
    move_z.finish()
    for copy in sends + asks + replies + returns:
        copy.wait_send()


def step(wanted, place, prefix, counts, fresh, beams, slots, hidden, gain, egain, *large):
    table, cached, w_self, w_query, w, w_cross = large
    chunk = pltpu.VMEM((LANES, 8, 512), f32)
    shape = jax.ShapeDtypeStruct(hidden.shape, bf16)
    return pl.pallas_call(
        step_kernel,
        out_shape=(shape, shape),
        in_specs=[SMEM] * 4 + [VMEM] * 6 + [ANY] * 6,
        out_specs=(VMEM, VMEM),
        scratch_shapes=[
            pltpu.VMEM((2, table.shape[0] // 10, HD), bf16),
            pltpu.VMEM(table.shape, f32),
            pltpu.VMEM((CAP, HD), f32),
            pltpu.VMEM((GROUPS, CAP, HD), bf16),
            pltpu.VMEM((GROUPS, CAP, HD), bf16),
            pltpu.VMEM((2, DE // 8, 2, 2 * HD), bf16),
            pltpu.VMEM((4, DE, 4 * HD), bf16),
            pltpu.VMEM((4, DE, 4 * HD), bf16),
            pltpu.VMEM(cached.shape, bf16),
            pltpu.VMEM(w_self.shape, bf16),
            pltpu.VMEM(w_query.shape, bf16),
            pltpu.VMEM((8, 2 * HD), f32),
        ]
        + [chunk] * 6
        + [
            pltpu.VMEM((2, 8, 256, HD), bf16),
            pltpu.VMEM((4, 2, 4, 256, HD), bf16),
            pltpu.VMEM((4, 2, 4, 256, HD), bf16),
            pltpu.VMEM((256, DE), bf16),
            pltpu.VMEM((2, 2, 4, 256, 4 * HD), bf16),
            pltpu.VMEM((GROUPS, 8, 2 * HD), f32),
            pltpu.VMEM((8, 2 * HD), f32),
            pltpu.VMEM((4, 8, 2 * HD), f32),
            pltpu.VMEM((4, 8, 2 * HD), f32),
            pltpu.VMEM((2, 4, 8, 2 * HD), f32),
            pltpu.VMEM((2, 4, 8, 2 * HD), f32),
            pltpu.VMEM((GROUPS, 8, 2 * HD), f32),
            DMA((2,)),
            DMA((2,)),
            DMA((4,)),
            DMA((7,)),
            DMA((7,)),
            DMA((4, 15)),
            DMA((4, 15)),
            DMA((4, 3)),
            DMA((4, 3)),
            [DMA((2, 3)), DMA((2, 3)), DMA((2, 3)), DMA((2, 3)), DMA((2,))],
            [DMA((2, 3)), DMA((2, 3)), DMA((2, 3)), DMA((2, 3)), DMA((2,))],
            DMA((7,)),
            DMA((7,)),
            DMA((2, 3)),
            DMA((2, 3)),
            DMA((2, 3)),
            DMA((2, 3)),
            DMA((7,)),
            DMA((7,)),
        ],
        compiler_params=params(0),
        name="step",
    )(wanted, place, prefix, counts, fresh, beams, slots, hidden, gain, egain, *large)


def local(
    neighbour_ids,
    neighbour_shard,
    neighbour_count,
    slot_beam,
    prefix_length,
    embed_table,
    encoder_gain,
    hidden_in,
    decoder_gain,
    fresh_projections,
    cached_pairs,
    w_self_out,
    w_query,
    w_pairs,
    w_cross_out,
):
    me = lax.axis_index("grp")
    shards = neighbour_shard.reshape(neighbour_ids.shape)
    wanted, place = prepare(neighbour_ids, shards, neighbour_count[:, None])
    fresh = jnp.transpose(fresh_projections.astype(f32), (1, 0, 2))
    slots = lax.dynamic_slice_in_dim(slot_beam, me * 8, 8)
    return step(
        wanted, place, prefix_length, neighbour_count, fresh, slot_beam[None, :], slots[:, None],
        hidden_in, decoder_gain[None, :], encoder_gain[None, :],
        embed_table, cached_pairs, w_self_out, w_query, w_pairs, w_cross_out,
    )


def solution(mesh):
    placed = (
        P(),
        P(),
        P(),
        P(),
        P("grp"),
        P("grp", "tp"),
        P(),
        P("grp", None),
        P(),
        P("grp", None, "tp"),
        P("grp", None, None, "tp"),
        P("tp", None),
        P(None, "tp"),
        P(None, None, "tp"),
        P("tp", None),
    )
    return jax.shard_map(
        local,
        mesh=mesh,
        in_specs=placed,
        out_specs=(P("grp", None), P("grp", None)),
        check_vma=False,
    )
```

time: 600 us -> 145 us (0.24)
  waiting for transfers between devices: 240 us -> 0 us
  blocking collectives: 149 us -> 0 us
  local copies, waits for them, and re-layouts: 143 us -> 5.9 us
  Pallas kernels: 0 us -> 137 us
  other arithmetic: 27 us -> 1.31 us
  matrix products: 23 us -> 0 us
  between operations: 15.7 us -> 0.65 us
    psum x2 -> x0, blocking collectives: 149 us -> none  [the longest x1 75 us: local(): lax.psum(jnp.dot(cross_attended, w_cross_out, preferred_element_type=jnp....]
    all_gather x2 -> x0, waiting for transfers between devices: 145 us -> none  [the longest x1 117 us: local(): lax.all_gather(flat_rows, 'tp', axis=1, tiled=True)]
    pallas_call x0 -> x2, Pallas kernels: none -> 137 us  [the longest x1 133 us: step(): pl.pallas_call(step_kernel, out_shape=(shape, shape), in_specs=[SMEM] * 4...]
    gather x2 -> x0, local copies, waits for them, and re-layouts: 116 us -> none  [the longest x1 112 us: dense_rows(): looked = jnp.take(embed_table, offset_ids.reshape(-1), axis=0)]
    reduce_scatter x1 -> x0, waiting for transfers between devices: 54.2 us -> none  [local(): lax.psum_scatter(partial_rows, 'grp', scatter_dimension=0, tiled=True)]
    psum x1 -> x0, waiting for transfers between devices: 41.1 us -> none  [local(): lax.psum(jnp.dot(attended, w_self_out, preferred_element_type=jnp.float32...]
    dot_general x8 -> x0, matrix products: 23 us -> none  [the longest x1 13.7 us: local(): jnp.dot(lax.all_gather(flat_rows, 'tp', axis=1, tiled=True), pair_matrix,...]
    select_n x4 -> x0, other arithmetic: 17.2 us -> none  [the longest x1 13.2 us: dense_rows(): return jnp.where(inside[:, None], looked, jnp.zeros_like(looked))]
  transfers between devices with their start and end apart: 4 -> 0, of which waited for: 4 -> 0; matrix products, arithmetic and copies ran while one was open for 5% -> 0% of each run, Pallas kernels for 0% -> 0%
where the time goes in v2:
time: 145 us
  Pallas kernels  137 us (94%)
  local copies, waits for them, and re-layouts  5.9 us (4%)
    pallas_call x1, Pallas kernels, step(): pl.pallas_call(step_kernel, out_shape=(shape, shape), in_specs=[SMEM] * 4...  133 us
    pallas_call x1, Pallas kernels, prepare(): pl.pallas_call(prep_kernel, out_shape=(jax.ShapeDtypeStruct((GROUPS, 32,...  3.6 us
    unnamed x2, local copies, waits for them, and re-layouts  3.14 us

profile of v2, /device:TPU:0, one launch (start us, length us, event | category | flops | bytes accessed | tf_op | source)
XLA Modules:
  0.0 144.7 jit_solution(14917394351869627565)
XLA Ops:
  0.6 0.7 dynamic-slice_bitcast_fusion
  1.4 0.7 copy.18.slots
  2.0 1.3 convert_bitcast_fusion.fresh
  3.4 1.4 copy.17.counts
  4.7 3.6 %prep.1 = (s32[8,32,32]{2,1,0:T(8,128)}, s32[32,128]{1,0:T(8,128)}) custom-call(s32[256,128]{1,0:T(8,128)} %ids.1, s32[256,128]{1,0:T(8,128)} %bitcast.9, s32[64,1]{1,0:T(8,128)} %copy.17.counts), custom_call_target="tpu_custom_call" | custom-call | tf_op jit(solution)/shard_map/prep/pallas_call | solution.py:122
  8.3 133.2 %step.1 = (bf16[8,8192]{1,0:T(8,128)(2,1)}, bf16[8,8192]{1,0:T(8,128)(2,1)}) custom-call(s32[8,32,32]{2,1,0:T(8,128)} %get-tuple-element.4.wanted, s32[32,128]{1,0:T(8,128)} %get-tuple-element.5.place, s32[8]{0:T(128)} %prefix.1, s32[64]{0:T(128)} %counts.1, f32[3,8,256]{2,1,0:T(8,128)} %convert_bitcast_fusion.fresh, s32[1,64]{1,0:T(1,128)} %bitcast.13, ...), custom_call_target="tpu_custom_call" | custom-call | tf_op jit(solution)/shard_map/step/pallas_call | solution.py:587
  141.5 1.6 %copy.21 = bf16[8,8192]{1,0:T(8,128)(2,1)} copy(bf16[8,8192]{1,0:T(8,128)(2,1)} %get-tuple-element.8) | data formatting | bytes 262144
  143.1 1.6 %copy.22 = bf16[8,8192]{1,0:T(8,128)(2,1)} copy(bf16[8,8192]{1,0:T(8,128)(2,1)} %get-tuple-element.9) | data formatting | bytes 262144

commit v3 on v2

v3 whole, which is shorter than its diff:
```python
import math

import jax
import jax.numpy as jnp
from jax import lax
from jax.experimental import pallas as pl
from jax.experimental.pallas import tpu as pltpu
from jax.sharding import PartitionSpec as P

MESH = pl.DeviceIdType.MESH
DMA = pltpu.SemaphoreType.DMA
VMEM = pl.BlockSpec(memory_space=pltpu.VMEM)
SMEM = pl.BlockSpec(memory_space=pltpu.SMEM)
ANY = pl.BlockSpec(memory_space=pl.ANY)

HD = 128
DE = 2048
NLEN = 128
KMAX = 4
CACHE = 512
CAP = 1024
GROUPS = 8
LANES = 16
ROOT = 1.0 / math.sqrt(HD)
epsilon = 1e-05
f32 = jnp.float32
bf16 = jnp.bfloat16
BIG = 62 * 2**20


def params(cid=None):
    if cid is None:
        return pltpu.CompilerParams(vmem_limit_bytes=BIG)
    return pltpu.CompilerParams(collective_id=cid, has_side_effects=True, vmem_limit_bytes=BIG)


def remote(src, dst, send, recv, where):
    return pltpu.make_async_remote_copy(
        src_ref=src, dst_ref=dst, send_sem=send, recv_sem=recv, device_id=where, device_id_type=MESH
    )


def head_rows(row):
    rows = lax.broadcasted_iota(jnp.int32, (8, 2 * HD), 0)
    lanes = lax.broadcasted_iota(jnp.int32, (8, 2 * HD), 1)
    return jnp.where(lanes // HD == rows, jnp.broadcast_to(row, (8, 2 * HD)), 0.0)


def head_pick(full):
    rows = lax.broadcasted_iota(jnp.int32, (8, 2 * HD), 0)
    lanes = lax.broadcasted_iota(jnp.int32, (8, 2 * HD), 1)
    return jnp.sum(jnp.where(lanes // HD == rows, full, 0.0), axis=0, keepdims=True)


def dot(a, b):
    return jnp.dot(a, b, preferred_element_type=f32)


def dot_t(a, b):
    return lax.dot_general(a, b, (((1,), (1,)), ((), ())), preferred_element_type=f32)


def prep_kernel(ids, shards, counts, wanted, place):
    me = lax.axis_index("grp")
    rows = lax.broadcasted_iota(jnp.int32, (256, 1), 0)
    beams = lax.broadcasted_iota(jnp.int32, (256, 64), 1)
    of_beam = lax.broadcasted_iota(jnp.int32, (256, 64), 0) // KMAX == beams
    held = jnp.sum(jnp.where(of_beam, counts[...], 0), axis=1, keepdims=True)
    alive = rows % KMAX < held
    upper = (
        lax.broadcasted_iota(jnp.int32, (NLEN, NLEN), 0)
        <= lax.broadcasted_iota(jnp.int32, (NLEN, NLEN), 1)
    ).astype(bf16)
    down = lax.broadcasted_iota(jnp.int32, (256, 256), 0)
    along = lax.broadcasted_iota(jnp.int32, (256, 256), 1)
    before = ((down // 32 == along // 32) & (along < down)).astype(bf16)
    ones = jnp.ones((NLEN, NLEN), bf16)

    def ranks(mask):
        mask = mask.astype(bf16)
        return dot(mask, upper) + dot(before, dot(mask, ones).astype(bf16)) - 1.0

    mine = (shards[...] == me) & alive
    rank = jnp.where(mine, ranks(mine), -1.0).astype(jnp.int32)
    high, low = rank >> 5, rank & 31
    high = jnp.where(mine, high, -1)
    id_high, id_low = (ids[...] >> 7).astype(f32), (ids[...] & 127).astype(f32)
    small = lax.broadcasted_iota(jnp.int32, (32, NLEN), 0)
    for g in range(GROUPS):
        left, right = [], []
        for i in range(32 * g, 32 * g + 32):
            left.append((small == high[i : i + 1]).astype(bf16))
            spot = small == low[i : i + 1]
            right.append(
                jnp.concatenate(
                    [
                        jnp.where(spot, id_high[i : i + 1], 0.0).astype(bf16),
                        jnp.where(spot, id_low[i : i + 1], 0.0).astype(bf16),
                    ],
                    axis=0,
                )
            )
        both = dot_t(jnp.concatenate(left, axis=1), jnp.concatenate(right, axis=1))
        wanted[g] = (both[:, :32] * 128.0 + both[:, 32:]).astype(jnp.int32)

    at = pl.ds(pl.multiple_of(me * 32, 32), 32)
    own = jnp.concatenate([shards[at, :]] * GROUPS, axis=0)
    beam = me * 8 + lax.broadcasted_iota(jnp.int32, (256, 64), 0) % 32 // KMAX
    own_held = jnp.sum(jnp.where(beam == beams, counts[...], 0), axis=1, keepdims=True)
    named = (own == rows // 32) & (rows % KMAX < own_held)
    spots = jnp.where(named, ranks(named) + (rows // 32 * CAP).astype(f32), 0.0).astype(jnp.int32)
    total = spots[0:32]
    for s in range(1, GROUPS):
        total = total + spots[32 * s : 32 * s + 32]
    place[...] = total


def prepare(ids, shards, counts):
    return pl.pallas_call(
        prep_kernel,
        out_shape=(
            jax.ShapeDtypeStruct((GROUPS, 32, 32), jnp.int32),
            jax.ShapeDtypeStruct((32, NLEN), jnp.int32),
        ),
        in_specs=[VMEM, VMEM, VMEM],
        out_specs=(VMEM, VMEM),
        compiler_params=params(),
        name="prep",
    )(ids, shards, counts)


class Ring:
    def __init__(self, out, here, peer, send, recv):
        up, down, far = lax.rem(here + 1, 4), lax.rem(here + 3, 4), lax.rem(here + 2, 4)
        low, high = pl.ds(0, DE // 2), pl.ds(DE // 2, DE // 2)

        def copy(k, shard, part, to):
            piece = out.at[shard, part]
            return remote(piece, piece, send.at[k], recv.at[k], peer(to))

        self.first = [copy(0, here, low, up), copy(1, here, high, down)]
        self.relays = [copy(2, down, low, up), copy(3, up, high, down)]
        self.second = [copy(4, here, high, up), copy(5, here, low, down)]

    def start(self):
        for copy in self.first:
            copy.start()

    def service(self):
        for copy, relay in zip(self.first, self.relays):
            copy.wait_recv()
            relay.start()
        for copy in self.second:
            copy.start()

    def finish(self):
        for copy in self.relays + self.second:
            copy.wait_recv()
        for copy in self.first + self.relays + self.second:
            copy.wait_send()


class Spread:
    def __init__(self, held, weights, part, red, full, sems):
        self.held, self.weights, self.part, self.red, self.full = held, weights, part, red, full
        self.psend, self.precv, self.asend, self.arecv = sems
        self.t = lax.axis_index("tp")

    def start(self):
        self.reduce = []
        for d in range(1, LANES + 1):
            p = lax.rem(self.t + d, LANES)
            at = pl.ds(pl.multiple_of(p * 512, 512), 512)
            self.part[p] = dot(self.held, self.weights[:, at])
            if d < LANES:
                copy = remote(
                    self.part.at[p], self.red.at[self.t],
                    self.psend.at[d - 1], self.precv.at[d - 1], {"tp": p},
                )
                copy.start()
                self.reduce.append(copy)

    def share(self):
        total = self.part[self.t]
        for d, copy in enumerate(self.reduce):
            copy.wait_recv()
            total = total + self.red[lax.rem(self.t + LANES - 1 - d, LANES)]
        self.full[self.t] = total
        self.shared = []
        for d in range(1, LANES):
            mine = self.full.at[self.t]
            copy = remote(
                mine, mine, self.asend.at[d - 1], self.arecv.at[d - 1],
                {"tp": lax.rem(self.t + d, LANES)},
            )
            copy.start()
            self.shared.append(copy)

    def arrive(self):
        for copy in self.shared:
            copy.wait_recv()

    def finish(self):
        for copy in self.reduce + self.shared:
            copy.wait_send()


class Move:
    def __init__(self, placed, out, core, a, b, peer_a, peer_b, sibling, sems):
        self.asend, self.arecv, self.bsend, self.brecv, self.own = sems
        self.placed, self.out, self.core, self.sibling = placed, out, core, sibling
        self.a, self.b, self.peer_a, self.peer_b = a, b, peer_a, peer_b
        self.exchanged, self.ups, self.downs, self.relays, self.kept = {}, {}, {}, {}, {}

    def exchange_own(self, h):
        a, b, first = self.a, self.b, self.core * 4
        line = []
        for d in (1, 3, 2):
            p = lax.rem(a + d, 4)
            copy = remote(
                self.placed.at[h, first + p], self.out.at[b, h, a, self.core],
                self.asend.at[h, d], self.arecv.at[h, d], self.peer_a(p),
            )
            copy.start()
            line.append(copy)
        self.exchanged[h] = self.exchanged.get(h, []) + line
        self.kept[h] = pltpu.make_async_copy(
            self.placed.at[h, first + a], self.out.at[b, h, a, self.core], self.own.at[h]
        )
        self.kept[h].start()

    def exchange_other(self, h):
        a, b, first = self.a, self.b, (1 - self.core) * 4
        line = []
        for d in (1, 3, 2, 0):
            p = lax.rem(b + d, 4)
            copy = remote(
                self.placed.at[h, first + p], self.out.at[a, h, b, self.core],
                self.asend.at[h, 4 + d], self.arecv.at[h, 4 + d],
                {"grp": self.sibling, **self.peer_b(p)},
            )
            copy.start()
            line.append(copy)
        self.exchanged[h] = self.exchanged.get(h, []) + line

    def gather(self, h):
        self.kept[h].wait()
        for copy in self.exchanged[h]:
            copy.wait_recv()
        mine = self.out.at[self.b, h]
        up, down = lax.rem(self.b + 1, 4), lax.rem(self.b + 3, 4)
        self.ups[h] = remote(
            mine, mine, self.bsend.at[h, 0], self.brecv.at[h, 0], self.peer_b(up)
        )
        self.downs[h] = remote(
            mine, mine, self.bsend.at[h, 1], self.brecv.at[h, 1], self.peer_b(down)
        )
        self.ups[h].start()
        self.downs[h].start()

    def relay(self, h):
        up, down = lax.rem(self.b + 1, 4), lax.rem(self.b + 3, 4)
        if h % 2 == 0:
            self.ups[h].wait_recv()
            piece, to = self.out.at[down, h], up
        else:
            self.downs[h].wait_recv()
            piece, to = self.out.at[up, h], down
        self.relays[h] = remote(
            piece, piece, self.bsend.at[h, 2], self.brecv.at[h, 2], self.peer_b(to)
        )
        self.relays[h].start()

    def arrive(self, h):
        (self.downs if h % 2 == 0 else self.ups)[h].wait_recv()
        self.relays[h].wait_recv()

    def finish(self):
        for h in self.ups:
            for copy in self.exchanged[h]:
                copy.wait_send()
            for copy in (self.ups[h], self.downs[h], self.relays[h]):
                copy.wait_send()


def step_kernel(
    wanted_in, place, prefix, counts, slots, fresh, beams, hidden, gain, egain,
    table, cached, w_self, w_query, w, w_cross,
    delta, out,
    wanted, tbuf, wide, found, rows, got, wbuf, wx, vc, vs, vq, attended,
    part, red, full, cpart, cred, cfull,
    placed, mb, enc, pairs, qall, qsent, qa, answers, ab, aall,
    tsem, wsem, lsem, ysend, yrecv, rsems, csems, rings, ringr, msems,
    qgsend, qgrecv, qtsend, qtrecv, atsend, atrecv, agsend, agrecv,
):
    g, t = lax.axis_index("grp"), lax.axis_index("tp")
    z, x = t // 4, lax.rem(t, 4)
    groups = [lax.rem(g + d, GROUPS) for d in range(1, GROUPS)]
    lanes = [lax.rem(t + d, LANES) for d in range(1, LANES)]
    core = lax.rem(g, 2)
    sibling = g + 1 - 2 * core
    a, b = x * (1 - core) + z * core, z * (1 - core) + x * core

    def by_a(p):
        return {"tp": p * (1 + 3 * core) + (1 - core) * z * 4 + core * x}

    def by_b(p):
        return {"tp": p * (4 - 3 * core) + (1 - core) * x + core * z * 4}

    peers = [{"grp": p} for p in groups] + [{"tp": p} for p in lanes]
    for d in range(1, 4):
        peers.append({"grp": sibling, **by_a(lax.rem(a + d, 4))})
        peers.append({"grp": sibling, **by_b(lax.rem(b + d, 4))})
    barrier = pltpu.get_barrier_semaphore()
    for peer in peers:
        pl.semaphore_signal(barrier, inc=1, device_id=peer, device_id_type=MESH)

    tstep, wstep = table.shape[0] // 10, DE // 8
    tload = [
        pltpu.make_async_copy(
            table.at[pl.ds(i * tstep, tstep)], tbuf.at[i % 5], tsem.at[i % 5]
        )
        for i in range(10)
    ]
    wload = [
        pltpu.make_async_copy(w.at[pl.ds(i * wstep, wstep)], wbuf.at[i % 4], wsem.at[i % 4])
        for i in range(8)
    ]
    loads = [
        pltpu.make_async_copy(cached, vc, lsem.at[0]),
        pltpu.make_async_copy(w_self, vs, lsem.at[1]),
        pltpu.make_async_copy(w_query, vq, lsem.at[2]),
    ]
    for copy in loads[:2]:
        copy.start()
    for i in range(4):
        wload[i].start()
    listed = pltpu.make_async_copy(wanted_in, wanted, lsem.at[4])
    listed.start()
    for i in range(5):
        tload[i].start()
    loads[0].wait()
    positions = lax.broadcasted_iota(jnp.int32, (8, CACHE), 1)
    for n in range(8):
        newest = fresh[n].astype(f32)
        spread = head_rows(newest[0:1])
        scores = dot_t(spread.astype(bf16), vc[n, 0]) * ROOT
        fresh_score = jnp.sum(spread * newest[1:2], axis=1, keepdims=True) * ROOT
        live = positions < prefix[n]
        top = jnp.maximum(
            jnp.max(jnp.where(live, scores, -jnp.inf), axis=1, keepdims=True), fresh_score
        )
        raised = jnp.where(live, jnp.exp(scores - top), 0.0)
        fresh_raised = jnp.exp(fresh_score - top)
        total = jnp.sum(raised, axis=1, keepdims=True) + fresh_raised
        weights = (raised / total).astype(bf16)
        fresh_weight = (fresh_raised / total).astype(bf16).astype(f32)
        mixed = dot(weights, vc[n, 1]) + fresh_weight * newest[2:3]
        attended[pl.ds(n, 1), :] = head_pick(mixed)
    loads[1].wait()
    pl.semaphore_wait(barrier, len(peers))
    own_sum = Spread(
        attended[...].astype(bf16), vs, part, red, full, [rsems.at[i] for i in range(4)]
    )
    own_sum.start()
    for i in range(8):
        wload[i].wait()
        flat = wbuf[i % 4].reshape(wstep, 512)
        at = pl.ds(i * wstep, wstep)
        wx[a, at, :] = flat
        if i + 4 < 8:
            wload[i + 4].start()
    ring = Ring(wx, a, by_a, rings, ringr)
    ring.start()
    loads[2].start()
    late = pltpu.make_async_copy(w_cross, vs, lsem.at[3])
    late.start()
    for i in range(10):
        tload[i].wait()
        wide[pl.ds(i * tstep, tstep), :] = tbuf[i % 5].astype(f32)
        if i + 5 < 10:
            tload[i + 5].start()

    def look(p):
        def some(k, c):
            for u in range(32):
                found[k * 32 + u, :] = wide[wanted[p * CAP + k * 32 + u], :]
            return c

        lax.fori_loop(0, CAP // 32, some, 0)
        return found[...].astype(bf16)

    sends = []

    def look_and_send(d):
        p = groups[d]
        rows[p] = look(p)
        copy = remote(rows.at[p], got.at[g], ysend.at[d], yrecv.at[d], {"grp": p})
        copy.start()
        sends.append(copy)

    listed.wait()
    for d in range(7):
        look_and_send(d)
        if d == 2:
            own_sum.share()
    ring.service()
    got[g] = look(g)
    own_sum.arrive()
    squares = jnp.zeros((8, 512), f32)
    for c in range(LANES):
        at = pl.ds(c * 512, 512)
        summed = full[c]
        delta[:, at] = summed.astype(bf16)
        r = hidden[:, at].astype(f32) + summed
        squares = squares + r * r
    scale = lax.rsqrt(jnp.sum(squares, axis=1, keepdims=True) / (LANES * 512) + epsilon)
    loads[2].wait()
    asked = jnp.zeros((8, 2 * HD), f32)
    for c in range(LANES):
        at = pl.ds(c * 512, 512)
        r = hidden[:, at].astype(f32) + full[c]
        normed = (r * scale * gain[:, at]).astype(bf16)
        asked = asked + dot(normed, vq[at, :])
    qall[g] = asked.astype(bf16).astype(f32)
    asks = []
    for d, p in enumerate(groups):
        copy = remote(qall.at[g], qall.at[g], qgsend.at[d], qgrecv.at[d], {"grp": p})
        copy.start()
        asks.append(copy)


    for copy in sends:
        copy.wait_recv()
    for s in range(GROUPS):
        wide[pl.ds(s * CAP, CAP), :] = got[s].astype(f32)

    def put(h, first):
        def beam(b, c):
            def some(k, c):
                line = (first + b) * 4 + h * 2 + k // 4
                column = lax.rem(k, 4) * 32
                for u in range(32):
                    found[k * 32 + u, :] = wide[place[line, column + u], :]
                return c

            lax.fori_loop(0, 8, some, 0)
            placed[h, first + b] = found[0:256, :].astype(bf16)
            return c

        lax.fori_loop(0, 4, beam, 0)

    move = Move(placed, mb, core, a, b, by_a, by_b, sibling, msems)
    put(0, 4 - 4 * core)
    move.exchange_other(0)
    put(0, 4 * core)
    move.exchange_own(0)
    put(1, 4 - 4 * core)
    put(1, 4 * core)
    move.gather(0)
    move.exchange_other(1)
    move.exchange_own(1)
    move.relay(0)
    move.gather(1)
    for copy in asks:
        copy.wait_recv()
    numbers = lax.broadcasted_iota(jnp.int32, (16, 64), 0) + (g - core) * 8
    chosen = (numbers == beams[...]).astype(bf16)
    routed = dot(chosen, qall[...].reshape(64, 2 * HD).astype(bf16))
    qsent[...] = routed
    qa[a] = routed
    for d in range(1, 4):
        copy = remote(
            qsent, qa.at[a], qtsend.at[d - 1], qtrecv.at[d - 1], by_a(lax.rem(a + d, 4))
        )
        copy.start()
        asks.append(copy)
    ring.finish()

    def encode(h, side):
        def piece(p):
            i, j = p // 4 * (1 - core) + p % 4 * core, p % 4 * (1 - core) + p // 4 * core
            return mb[i, h, j, side]

        squares = jnp.zeros((256, HD), f32)
        for p in range(LANES):
            value = piece(p).astype(f32)
            squares = squares + value * value
        scale = lax.rsqrt(jnp.sum(squares, axis=1, keepdims=True) / DE + epsilon)
        for p in range(LANES):
            at = pl.ds(p * HD, HD)
            enc[:, at] = (piece(p).astype(f32) * scale * egain[:, at]).astype(bf16)

        def project(k, carry):
            pairs[side, h, k] = dot(enc[...], wx[k]).astype(bf16)
            return carry

        lax.fori_loop(0, 4, project, 0)

    tokens = lax.broadcasted_iota(jnp.int32, (8, KMAX * NLEN), 1)

    def attend(side):
        beam = side * 8 + core * 4 + a
        live = tokens < counts[(g - core) * 8 + beam] * NLEN
        for k in range(4):
            spread = head_rows(qa[k, pl.ds(beam, 1), :]).astype(bf16)
            scores = jnp.concatenate(
                [dot_t(spread, pairs[side, h, k, :, : 2 * HD]) for h in range(2)], axis=1
            )
            scores = jnp.where(live, scores * ROOT, -jnp.inf)
            raised = jnp.exp(scores - jnp.max(scores, axis=1, keepdims=True))
            weights = (raised / jnp.sum(raised, axis=1, keepdims=True)).astype(bf16)
            mixed = dot(weights[:, :256], pairs[side, 0, k, :, 2 * HD :])
            mixed = mixed + dot(weights[:, 256:], pairs[side, 1, k, :, 2 * HD :])
            answer = head_pick(mixed).astype(bf16).astype(f32)
            answers[k, pl.ds(side, 1), :] = answer

    move.arrive(0)
    encode(0, 0)
    move.relay(1)
    encode(0, 1)
    for copy in asks[7:]:
        copy.wait_recv()
    move.arrive(1)
    encode(1, 0)
    attend(0)
    encode(1, 1)
    attend(1)
    replies = []
    for d in range(1, 4):
        p = lax.rem(a + d, 4)
        copy = remote(answers.at[p], ab.at[a], atsend.at[d - 1], atrecv.at[d - 1], by_a(p))
        copy.start()
        replies.append(copy)
    ab[a] = answers[a]
    for copy in replies:
        copy.wait_recv()
    aall[g] = jnp.concatenate([ab[k, 0:2] for k in range(4)], axis=0)
    returns = []
    for d, p in enumerate(groups):
        copy = remote(aall.at[g], aall.at[g], agsend.at[d], agrecv.at[d], {"grp": p})
        copy.start()
        returns.append(copy)
    late.wait()
    for copy in returns:
        copy.wait_recv()
    line = lax.broadcasted_iota(jnp.int32, (8, 64), 0)
    decoded = jnp.zeros((8, 64), jnp.int32)
    for j in range(8):
        beam = slots[g * 8 + j]
        held_at = (beam // 16 * 2 + beam // 4 % 2) * 8 + beam % 4 * 2 + beam // 8 % 2
        decoded = jnp.where(line == j, held_at, decoded)
    picks = (lax.broadcasted_iota(jnp.int32, (8, 64), 1) == decoded).astype(bf16)
    held = dot(picks, aall[...].reshape(64, 2 * HD).astype(bf16)).astype(bf16)
    cross_sum = Spread(held, vs, cpart, cred, cfull, [csems.at[i] for i in range(4)])
    cross_sum.start()
    cross_sum.share()
    cross_sum.arrive()
    for c in range(LANES):
        out[:, pl.ds(c * 512, 512)] = cfull[c].astype(bf16)
    own_sum.finish()
    cross_sum.finish()
    move.finish()
    for copy in sends + asks + replies + returns:
        copy.wait_send()


def step(wanted, place, prefix, counts, slots, fresh, beams, hidden, gain, egain, *large):
    table, cached, w_self, w_query, w, w_cross = large
    chunk = pltpu.VMEM((LANES, 8, 512), f32)
    shape = jax.ShapeDtypeStruct(hidden.shape, bf16)
    return pl.pallas_call(
        step_kernel,
        out_shape=(shape, shape),
        in_specs=[ANY] + [SMEM] * 4 + [VMEM] * 5 + [ANY] * 6,
        out_specs=(VMEM, VMEM),
        scratch_shapes=[
            pltpu.SMEM((GROUPS * CAP,), jnp.int32),
            pltpu.VMEM((5, table.shape[0] // 10, HD), bf16),
            pltpu.VMEM(table.shape, f32),
            pltpu.VMEM((CAP, HD), f32),
            pltpu.VMEM((GROUPS, CAP, HD), bf16),
            pltpu.VMEM((GROUPS, CAP, HD), bf16),
            pltpu.VMEM((4, DE // 8, 2, 2 * HD), bf16),
            pltpu.VMEM((4, DE, 4 * HD), bf16),
            pltpu.VMEM(cached.shape, bf16),
            pltpu.VMEM(w_self.shape, bf16),
            pltpu.VMEM(w_query.shape, bf16),
            pltpu.VMEM((8, 2 * HD), f32),
        ]
        + [chunk] * 6
        + [
            pltpu.VMEM((2, 8, 256, HD), bf16),
            pltpu.VMEM((4, 2, 4, 2, 256, HD), bf16),
            pltpu.VMEM((256, DE), bf16),
            pltpu.VMEM((2, 2, 4, 256, 4 * HD), bf16),
            pltpu.VMEM((GROUPS, 8, 2 * HD), f32),
            pltpu.VMEM((16, 2 * HD), f32),
            pltpu.VMEM((4, 16, 2 * HD), f32),
            pltpu.VMEM((4, 8, 2 * HD), f32),
            pltpu.VMEM((4, 8, 2 * HD), f32),
            pltpu.VMEM((GROUPS, 8, 2 * HD), f32),
            DMA((5,)),
            DMA((4,)),
            DMA((5,)),
            DMA((7,)),
            DMA((7,)),
            DMA((4, 15)),
            DMA((4, 15)),
            DMA((6,)),
            DMA((6,)),
            [DMA((2, 8)), DMA((2, 8)), DMA((2, 3)), DMA((2, 3)), DMA((2,))],
            DMA((7,)),
            DMA((7,)),
            DMA((3,)),
            DMA((3,)),
            DMA((3,)),
            DMA((3,)),
            DMA((7,)),
            DMA((7,)),
        ],
        compiler_params=params(0),
        name="step",
    )(wanted, place, prefix, counts, slots, fresh, beams, hidden, gain, egain, *large)


def hand_kernel(delta, out, delta_out, out_out):
    delta_out[...] = delta[...]
    out_out[...] = out[...]


def hand_over(delta, out):
    return pl.pallas_call(
        hand_kernel,
        out_shape=(jax.ShapeDtypeStruct(delta.shape, bf16),) * 2,
        in_specs=[VMEM, VMEM],
        out_specs=(VMEM, VMEM),
        name="hand_over",
    )(delta, out)


def local(
    neighbour_ids,
    neighbour_shard,
    neighbour_count,
    slot_beam,
    prefix_length,
    embed_table,
    encoder_gain,
    hidden_in,
    decoder_gain,
    fresh_projections,
    cached_pairs,
    w_self_out,
    w_query,
    w_pairs,
    w_cross_out,
):
    shards = neighbour_shard.reshape(neighbour_ids.shape)
    wanted, place = prepare(neighbour_ids, shards, neighbour_count[None, :])
    wanted = wanted.reshape(GROUPS * CAP)
    delta, out = step(
        wanted, place, prefix_length, neighbour_count, slot_beam, fresh_projections,
        slot_beam[None, :],        hidden_in, decoder_gain[None, :], encoder_gain[None, :],
        embed_table, cached_pairs, w_self_out, w_query, w_pairs, w_cross_out,
    )
    return hand_over(delta, out)


def solution(mesh):
    placed = (
        P(),
        P(),
        P(),
        P(),
        P("grp"),
        P("grp", "tp"),
        P(),
        P("grp", None),
        P(),
        P("grp", None, "tp"),
        P("grp", None, None, "tp"),
        P("tp", None),
        P(None, "tp"),
        P(None, None, "tp"),
        P("tp", None),
    )
    return jax.shard_map(
        local,
        mesh=mesh,
        in_specs=placed,
        out_specs=(P("grp", None), P("grp", None)),
        check_vma=False,
    )
```

time: 145 us -> 130 us (0.90)
  Pallas kernels: 137 us -> 127 us
  local copies, waits for them, and re-layouts: 5.9 us -> 2.92 us
    pallas_call x1 -> x2, Pallas kernels: 133 us -> 123 us  [the longest x1 121 us: step(): pl.pallas_call(step_kernel, out_shape=(shape, shape), in_specs=[ANY] + [S...]
    broadcast_in_dim x3 -> x0, local copies, waits for them, and re-layouts: 2.76 us -> none  [the longest x2 1.4 us: local(): slots[:, None]]
    unnamed x2 -> x1, local copies, waits for them, and re-layouts: 3.14 us -> 1.31 us
    reshape x0 -> x1, local copies, waits for them, and re-layouts: none -> 1.61 us  [local(): wanted = wanted.reshape(GROUPS * CAP)]
where the time goes in v3:
time: 130 us
  Pallas kernels  127 us (98%)
  local copies, waits for them, and re-layouts  2.92 us (2%)
    pallas_call x1, Pallas kernels, step(): pl.pallas_call(step_kernel, out_shape=(shape, shape), in_specs=[ANY] + [S...  121 us
    pallas_call x1, Pallas kernels, prepare(): pl.pallas_call(prep_kernel, out_shape=(jax.ShapeDtypeStruct((GROUPS, 32,...  3.45 us

profile of v3, /device:TPU:0, one launch (start us, length us, event | category | flops | bytes accessed | tf_op | source)
XLA Modules:
  0.0 130.1 jit_solution(4102699676632838626)
XLA Ops:
  0.6 1.3 %copy.17.fresh = bf16[8,3,256]{2,1,0:T(4,128)(2,1)} copy(bf16[8,3,256]{2,0,1:T(8,128)(2,1)} %param.24) | data formatting | bytes 24576 | tf_op args[9]
  1.9 3.4 %prep.1 = (s32[8,32,32]{2,1,0:T(8,128)}, s32[32,128]{1,0:T(8,128)}) custom-call(s32[256,128]{1,0:T(8,128)} %ids.1, s32[256,128]{1,0:T(8,128)} %bitcast.5, s32[1,64]{1,0:T(1,128)} %bitcast.8), custom_call_target="tpu_custom_call" | custom-call | tf_op jit(solution)/shard_map/prep/pallas_call | solution.py:119
  5.4 1.6 %reshape.11.wanted_in = s32[8192]{0:T(1024)} reshape(s32[8,32,32]{2,1,0:T(8,128)} %get-tuple-element.6) | data formatting | bytes 65536 | tf_op jit(solution)/shard_map/reshape | solution.py:661
  7.0 121.4 %step.1 = (bf16[8,8192]{1,0:T(8,128)(2,1)}, bf16[8,8192]{1,0:T(8,128)(2,1)}) custom-call(s32[8192]{0:T(1024)} %reshape.11.wanted_in, s32[32,128]{1,0:T(8,128)} %get-tuple-element.7.place, s32[8]{0:T(128)} %prefix.1, s32[64]{0:T(128)} %counts.1, s32[64]{0:T(128)} %slots.1, bf16[8,3,256]{2,1,0:T(4,128)(2,1)} %copy.17.fresh, s32[1,64]{1,0:T(1,128)} %bitcast.9, ...), custom_call_target="tpu_custom_call" | custom-call | tf_op jit(solution)/shard_map/step/pallas_call | solution.py:572
  128.5 1.7 %hand_over.1 = (bf16[8,8192]{1,0:T(8,128)(2,1)}, bf16[8,8192]{1,0:T(8,128)(2,1)}) custom-call(bf16[8,8192]{1,0:T(8,128)(2,1)} %get-tuple-element.8.delta, bf16[8,8192]{1,0:T(8,128)(2,1)} %get-tuple-element.9.out), custom_call_target="tpu_custom_call" | custom-call | tf_op jit(solution)/shard_map/hand_over/pallas_call | solution.py:633

commit v4 on v3

--- a/solution.py
+++ b/solution.py
@@ -143,15 +143,13 @@
         self.second = [copy(4, here, high, up), copy(5, here, low, down)]
 
     def start(self):
-        for copy in self.first:
+        for copy in self.first + self.second:
             copy.start()
 
     def service(self):
         for copy, relay in zip(self.first, self.relays):
             copy.wait_recv()
             relay.start()
-        for copy in self.second:
-            copy.start()
 
     def finish(self):
         for copy in self.relays + self.second:
@@ -185,6 +183,8 @@
         for d, copy in enumerate(self.reduce):
             copy.wait_recv()
             total = total + self.red[lax.rem(self.t + LANES - 1 - d, LANES)]
+        if self.full.dtype == bf16:
+            total = jnp.concatenate([total[:, :256], total[:, 256:]], axis=0).astype(bf16)
         self.full[self.t] = total
         self.shared = []
         for d in range(1, LANES):
@@ -456,12 +456,13 @@
     put(0, 4 * core)
     move.exchange_own(0)
     put(1, 4 - 4 * core)
+    move.exchange_other(1)
+    move.gather(0)
     put(1, 4 * core)
-    move.gather(0)
-    move.exchange_other(1)
     move.exchange_own(1)
     move.relay(0)
     move.gather(1)
+    move.relay(1)
     for copy in asks:
         copy.wait_recv()
     numbers = lax.broadcasted_iota(jnp.int32, (16, 64), 0) + (g - core) * 8
@@ -517,7 +518,6 @@
 
     move.arrive(0)
     encode(0, 0)
-    move.relay(1)
     encode(0, 1)
     for copy in asks[7:]:
         copy.wait_recv()
@@ -557,7 +557,9 @@
     cross_sum.share()
     cross_sum.arrive()
     for c in range(LANES):
-        out[:, pl.ds(c * 512, 512)] = cfull[c].astype(bf16)
+        both = cfull[c].astype(f32)
+        out[:, pl.ds(c * 512, 256)] = both[:8].astype(bf16)
+        out[:, pl.ds(c * 512 + 256, 256)] = both[8:].astype(bf16)
     own_sum.finish()
     cross_sum.finish()
     move.finish()
@@ -588,8 +590,9 @@
             pltpu.VMEM(w_query.shape, bf16),
             pltpu.VMEM((8, 2 * HD), f32),
         ]
-        + [chunk] * 6
+        + [chunk] * 5
         + [
+            pltpu.VMEM((LANES, 16, 256), bf16),
             pltpu.VMEM((2, 8, 256, HD), bf16),
             pltpu.VMEM((4, 2, 4, 2, 256, HD), bf16),
             pltpu.VMEM((256, DE), bf16),

time: 130 us -> 125 us (0.962)
  Pallas kernels: 127 us -> 121 us
    pallas_call x1, Pallas kernels: 121 us -> 116 us  [step(): pl.pallas_call(step_kernel, out_shape=(shape, shape), in_specs=[ANY] + [S...]
where the time goes in v4:
time: 125 us
  Pallas kernels  121 us (97%)
  local copies, waits for them, and re-layouts  2.92 us (2%)
    pallas_call x1, Pallas kernels, step(): pl.pallas_call(step_kernel, out_shape=(shape, shape), in_specs=[ANY] + [S...  116 us
    pallas_call x1, Pallas kernels, prepare(): pl.pallas_call(prep_kernel, out_shape=(jax.ShapeDtypeStruct((GROUPS, 32,...  3.45 us

profile of v4, /device:TPU:0, one launch (start us, length us, event | category | flops | bytes accessed | tf_op | source)
XLA Modules:
  0.0 124.8 jit_solution(11513199854300058589)
XLA Ops:
  0.6 1.3 %copy.17.fresh = bf16[8,3,256]{2,1,0:T(4,128)(2,1)} copy(bf16[8,3,256]{2,0,1:T(8,128)(2,1)} %param.24) | data formatting | bytes 24576 | tf_op args[9]
  1.9 3.4 %prep.1 = (s32[8,32,32]{2,1,0:T(8,128)}, s32[32,128]{1,0:T(8,128)}) custom-call(s32[256,128]{1,0:T(8,128)} %ids.1, s32[256,128]{1,0:T(8,128)} %bitcast.5, s32[1,64]{1,0:T(1,128)} %bitcast.8), custom_call_target="tpu_custom_call" | custom-call | tf_op jit(solution)/shard_map/prep/pallas_call | solution.py:119
  5.4 1.6 %reshape.11.wanted_in = s32[8192]{0:T(1024)} reshape(s32[8,32,32]{2,1,0:T(8,128)} %get-tuple-element.6) | data formatting | bytes 65536 | tf_op jit(solution)/shard_map/reshape | solution.py:664
  7.0 116.1 %step.1 = (bf16[8,8192]{1,0:T(8,128)(2,1)}, bf16[8,8192]{1,0:T(8,128)(2,1)}) custom-call(s32[8192]{0:T(1024)} %reshape.11.wanted_in, s32[32,128]{1,0:T(8,128)} %get-tuple-element.7.place, s32[8]{0:T(128)} %prefix.1, s32[64]{0:T(128)} %counts.1, s32[64]{0:T(128)} %slots.1, bf16[8,3,256]{2,1,0:T(4,128)(2,1)} %copy.17.fresh, s32[1,64]{1,0:T(1,128)} %bitcast.9, ...), custom_call_target="tpu_custom_call" | custom-call | tf_op jit(solution)/shard_map/step/pallas_call | solution.py:574
  123.1 1.7 %hand_over.1 = (bf16[8,8192]{1,0:T(8,128)(2,1)}, bf16[8,8192]{1,0:T(8,128)(2,1)}) custom-call(bf16[8,8192]{1,0:T(8,128)(2,1)} %get-tuple-element.8.delta, bf16[8,8192]{1,0:T(8,128)(2,1)} %get-tuple-element.9.out), custom_call_target="tpu_custom_call" | custom-call | tf_op jit(solution)/shard_map/hand_over/pallas_call | solution.py:636

commit v5 on v4

--- a/solution.py
+++ b/solution.py
@@ -384,7 +384,7 @@
     def look(p):
         def some(k, c):
             for u in range(32):
-                found[k * 32 + u, :] = wide[wanted[p * CAP + k * 32 + u], :]
+                found[k * 32 + u, :] = wide[wanted[p, k, u], :]
             return c
 
         lax.fori_loop(0, CAP // 32, some, 0)
@@ -577,7 +577,7 @@
         in_specs=[ANY] + [SMEM] * 4 + [VMEM] * 5 + [ANY] * 6,
         out_specs=(VMEM, VMEM),
         scratch_shapes=[
-            pltpu.SMEM((GROUPS * CAP,), jnp.int32),
+            pltpu.SMEM((GROUPS, 32, 32), jnp.int32),
             pltpu.VMEM((5, table.shape[0] // 10, HD), bf16),
             pltpu.VMEM(table.shape, f32),
             pltpu.VMEM((CAP, HD), f32),
@@ -661,7 +661,6 @@
 ):
     shards = neighbour_shard.reshape(neighbour_ids.shape)
     wanted, place = prepare(neighbour_ids, shards, neighbour_count[None, :])
-    wanted = wanted.reshape(GROUPS * CAP)
     delta, out = step(
         wanted, place, prefix_length, neighbour_count, slot_beam, fresh_projections,
         slot_beam[None, :],        hidden_in, decoder_gain[None, :], encoder_gain[None, :],

time: 125 us -> 124 us (level)
  local copies, waits for them, and re-layouts: 2.92 us -> 1.32 us
    reshape x1 -> x0, local copies, waits for them, and re-layouts: 1.61 us -> none  [local(): wanted = wanted.reshape(GROUPS * CAP)]
where the time goes in v5:
time: 124 us; the launch traced here: 123 us
  Pallas kernels  121 us (98%)
  local copies, waits for them, and re-layouts  1.32 us (1%)
    pallas_call x1, Pallas kernels, step(): pl.pallas_call(step_kernel, out_shape=(shape, shape), in_specs=[ANY] + [S...  116 us
    pallas_call x1, Pallas kernels, prepare(): pl.pallas_call(prep_kernel, out_shape=(jax.ShapeDtypeStruct((GROUPS, 32,...  3.45 us

profile of v5, /device:TPU:0, one launch (start us, length us, event | category | flops | bytes accessed | tf_op | source)
XLA Modules:
  0.0 123.2 jit_solution(10160826961400575981)
XLA Ops:
  0.6 1.3 %copy.17.fresh = bf16[8,3,256]{2,1,0:T(4,128)(2,1)} copy(bf16[8,3,256]{2,0,1:T(8,128)(2,1)} %param.24) | data formatting | bytes 24576 | tf_op args[9]
  1.9 3.5 %prep.1 = (s32[8,32,32]{2,1,0:T(8,128)}, s32[32,128]{1,0:T(8,128)}) custom-call(s32[256,128]{1,0:T(8,128)} %ids.1, s32[256,128]{1,0:T(8,128)} %bitcast.5, s32[1,64]{1,0:T(1,128)} %bitcast.8), custom_call_target="tpu_custom_call" | custom-call | tf_op jit(solution)/shard_map/prep/pallas_call | solution.py:119
  5.4 116.1 %step.1 = (bf16[8,8192]{1,0:T(8,128)(2,1)}, bf16[8,8192]{1,0:T(8,128)(2,1)}) custom-call(s32[8,32,32]{2,1,0:T(8,128)} %get-tuple-element.6.wanted_in, s32[32,128]{1,0:T(8,128)} %get-tuple-element.7.place, s32[8]{0:T(128)} %prefix.1, s32[64]{0:T(128)} %counts.1, s32[64]{0:T(128)} %slots.1, bf16[8,3,256]{2,1,0:T(4,128)(2,1)} %copy.17.fresh, s32[1,64]{1,0:T(1,128)} %bitcast.9, ...), custom_call_target="tpu_custom_call" | custom-call | tf_op jit(solution)/shard_map/step/pallas_call | solution.py:574
  121.5 1.7 %hand_over.1 = (bf16[8,8192]{1,0:T(8,128)(2,1)}, bf16[8,8192]{1,0:T(8,128)(2,1)}) custom-call(bf16[8,8192]{1,0:T(8,128)(2,1)} %get-tuple-element.8.delta, bf16[8,8192]{1,0:T(8,128)(2,1)} %get-tuple-element.9.out), custom_call_target="tpu_custom_call" | custom-call | tf_op jit(solution)/shard_map/hand_over/pallas_call | solution.py:636
